TPU v7x, 512 devices: a whole 4x8x8 slice. The times are simulated.
512 devices in a mesh: row: 16 (over x, y_lo, core), col: 32 (over y_hi, z).
Axes of the slice: x: 4, y: 8 (y_hi: 4, y_lo: 2; y = y_hi * 2 + y_lo), z: 8, core: 2. Of those that a mesh axis runs over, the one named last changes fastest.
Arguments:
- specimen: float32 [2, 4096, 8192], P(None, 'row', 'col'), may hold values from -6 to 6
- probe_field: float32 [2, 256, 256], replicated, may hold values from -5 to 5
- offsets: int32 [16, 32, 3, 2], P('row', 'col'), may hold values from -128 to 128
- amplitudes: float32 [16, 32, 3, 256, 256], P('row', 'col'), may hold values from 0.5 to 2.5
Outputs:
- updated: float32 [2, 4096, 8192], P(None, 'row', 'col')
Inputs may be any that keep to these rules, and one draw needn't show every extreme that they name: Window p of tile (r, c) starts at row r * 256 + offsets[r, c, p, 0] and column c * 256 + offsets[r, c, p, 1]; windows may reach past the specimen's border, where the object is zero.
All inputs are finite; a program needn't handle non-finite values.
Results may differ from a plain program's by a relative error of at most 0.0003.
Values sent between devices are 32-bit elements; how exact they have to be, the bound alone decides.
A program may use at most 64 MiB of HBM per device.

v0:
```python
import math

import jax
import jax.numpy as jnp
from jax import lax
from jax.sharding import PartitionSpec as P

WIN = 256
HALO = 128
ITERS = 2


smooth_term = 0.25
ridge_share = 0.1


def from_behind(block, axis, distance):
    devices = range(lax.axis_size(axis))
    route = [(i - distance, i) for i in devices if i - distance in devices]
    return lax.ppermute(block, axis, route)


def padded(cells, sides, width):
    for axis, dim in sides:
        count = lax.axis_size(axis)
        ends = count - 1
        head = lax.slice_in_dim(cells, 0, width, axis=dim)
        tail = lax.slice_in_dim(cells, cells.shape[dim] - width, cells.shape[dim], axis=dim)
        cells = jnp.concatenate(
            [
                lax.ppermute(tail, axis, [(i, (i + 1) % count) for i in range(ends)]),
                cells,
                lax.ppermute(head, axis, [((i + 1) % count, i) for i in range(ends)]),
            ],
            axis=dim,
        )
    return cells


def dft_tables(length):
    counter = jnp.arange(length, dtype=jnp.int32)
    product = counter[:, None] * counter[None, :] % length
    angle = product.astype(jnp.float32) * (2.0 * math.pi / length)
    scale = 1.0 / math.sqrt(length)
    return (jnp.cos(angle) * scale, -jnp.sin(angle) * scale)


def mat_left(matrix, stacked):
    return jnp.einsum("kn,pnm->pkm", matrix, stacked, precision=lax.Precision.HIGHEST)


def mat_right(stacked, matrix):
    return jnp.einsum("pnm,mk->pnk", stacked, matrix, precision=lax.Precision.HIGHEST)


def transform(cos_table, sin_table, real_part, imag_part):
    real_mid = mat_left(cos_table, real_part) - mat_left(sin_table, imag_part)
    imag_mid = mat_left(cos_table, imag_part) + mat_left(sin_table, real_part)
    real_out = mat_right(real_mid, cos_table) - mat_right(imag_mid, sin_table)
    imag_out = mat_right(imag_mid, cos_table) + mat_right(real_mid, sin_table)
    return (real_out, imag_out)


def window_gradient(probe_field, patch_real, patch_imag, amplitude, cos_table, sin_table):
    probe_real = probe_field[0]
    probe_imag = probe_field[1]
    exit_real = probe_real * patch_real - probe_imag * patch_imag
    exit_imag = probe_real * patch_imag + probe_imag * patch_real
    far_real, far_imag = transform(cos_table, sin_table, exit_real, exit_imag)
    modulus = jnp.sqrt(far_real * far_real + far_imag * far_imag + smooth_term)
    factor = 1.0 - amplitude / modulus
    back_real, back_imag = transform(cos_table, -sin_table, factor * far_real, factor * far_imag)
    grad_real = probe_real * back_real + probe_imag * back_imag
    grad_imag = probe_real * back_imag - probe_imag * back_real
    return (grad_real, grad_imag)


def add_window(total, piece, top, left):
    zero_index = jnp.zeros((), jnp.int32)
    block = lax.dynamic_slice(total, (zero_index, top, left), piece.shape)
    return lax.dynamic_update_slice(total, block + piece, (zero_index, top, left))


def add_band(total, band, start, axis_dim):
    current = lax.slice_in_dim(total, start, start + band.shape[axis_dim], axis=axis_dim)
    return lax.dynamic_update_slice_in_dim(total, current + band, start, axis_dim)


def fold_edges(stacked, rim_depth):
    span_size = stacked.shape[2]
    tile_size = span_size - 2 * HALO
    from_right = from_behind(stacked[:, :, :rim_depth], "col", -1)
    from_left = from_behind(stacked[:, :, span_size - rim_depth :], "col", 1)
    stacked = add_band(stacked, from_right, tile_size, 2)
    stacked = add_band(stacked, from_left, 2 * HALO - rim_depth, 2)
    from_below = from_behind(stacked[:, :rim_depth, :], "row", -1)
    from_above = from_behind(stacked[:, span_size - rim_depth :, :], "row", 1)
    stacked = add_band(stacked, from_below, tile_size, 1)
    stacked = add_band(stacked, from_above, 2 * HALO - rim_depth, 1)
    return stacked


def widen(core_tile):
    return padded(core_tile, (("row", 1), ("col", 2)), HALO)


def owned_peak(light_sum, tile_size):
    local_peak = jnp.max(light_sum[0, HALO : HALO + tile_size, HALO : HALO + tile_size])
    return lax.pmax(local_peak, ("row", "col"))


def local(specimen, probe_field, offsets, amplitudes):
    tile_size = specimen.shape[1]
    span_size = tile_size + 2 * HALO
    cos_table, sin_table = dft_tables(WIN)
    own_offsets = offsets[0, 0] + HALO
    own_amplitude = amplitudes[0, 0]
    window_count = own_offsets.shape[0]
    zero_index = jnp.zeros((), jnp.int32)
    intensity = probe_field[0] * probe_field[0] + probe_field[1] * probe_field[1]
    light_local = jnp.zeros((1, span_size, span_size), jnp.float32)
    for position in range(window_count):
        light_local = add_window(
            light_local, intensity[None], own_offsets[position, 0], own_offsets[position, 1]
        )
    rim_depth = HALO
    light_sum = fold_edges(light_local, rim_depth)
    light_peak = owned_peak(light_sum, tile_size)
    widened = widen(specimen)
    core_tile = specimen
    for iteration in range(ITERS):
        patches = jnp.stack(
            [
                lax.dynamic_slice(
                    widened,
                    (zero_index, own_offsets[position, 0], own_offsets[position, 1]),
                    (2, WIN, WIN),
                )
                for position in range(window_count)
            ]
        )
        grad_real, grad_imag = window_gradient(
            probe_field, patches[:, 0], patches[:, 1], own_amplitude, cos_table, sin_table
        )
        grad_local = jnp.zeros((2, span_size, span_size), jnp.float32)
        for position in range(window_count):
            piece = jnp.stack([grad_real[position], grad_imag[position]])
            grad_local = add_window(
                grad_local, piece, own_offsets[position, 0], own_offsets[position, 1]
            )
        gradient = fold_edges(grad_local, rim_depth)
        divisor = light_sum + ridge_share * light_peak
        inner_grad = gradient[:, HALO : HALO + tile_size, HALO : HALO + tile_size]
        inner_div = divisor[:, HALO : HALO + tile_size, HALO : HALO + tile_size]
        core_tile = (
            widened[:, HALO : HALO + tile_size, HALO : HALO + tile_size] - inner_grad / inner_div
        )
        if iteration + 1 < ITERS:
            widened = widen(core_tile)
    return core_tile


def solution(mesh):
    return jax.shard_map(
        local,
        mesh=mesh,
        in_specs=(
            P(None, "row", "col"),
            P(),
            P("row", "col", None, None),
            P("row", "col", None, None, None),
        ),
        out_specs=P(None, "row", "col"),
        check_vma=False,
    )
```

profile of v0, /device:TPU:36, one launch (start us, length us, event | category | flops | bytes accessed | tf_op | source)
XLA Modules:
  0.0 503.9 jit_solution(1603336797493579175)
XLA Ops:
  3.0 4.7 collective-permute-start.1
  11.7 4.3 collective-permute-start.2
  16.0 8.4 %collective-permute-start.3 = (f32[2,512,128]{2,1,0:T(8,128)S(1)}, f32[2,512,128]{2,1,0:T(8,128)}, u32[]{:S(2)}, u32[]{:S(2)}) collective-permute-start(f32[2,512,128]{2,1,0:T(8,128)S(1)} %get-tuple-element.30), channel_id=1, source_target_pairs={{1,0},{2,1},{3,2},{4,3},{5,4},{6,5},{7,6},{8,7},{9,8},{10,9},{11,1... | collective-permute-start | bytes 1572872 | tf_op jit(solution)/shard_map/ppermute | solution.py:33
  36.5 11.4 %collective-permute-done.3 = f32[2,512,128]{2,1,0:T(8,128)} collective-permute-done((f32[2,512,128]{2,1,0:T(8,128)S(1)}, f32[2,512,128]{2,1,0:T(8,128)}, u32[]{:S(2)}, u32[]{:S(2)}) %collective-permute-start.3) | collective-permute-done | bytes 524320 | tf_op jit(solution)/shard_map/ppermute | solution.py:33
  59.3 2.7 fusion.7
  90.3 7.5 %dynamic_update_slice.63 = f32[2,512,512]{2,1,0:T(8,128)S(1)} dynamic-update-slice(f32[2,512,512]{2,1,0:T(8,128)S(1)} %broadcast.23.clone, f32[2,256,256]{2,1,0:T(8,128)} %pad_maximum_fusion.5, s32[]{:T(128)} %constant.14.clone.1, s32[]{:T(128)S(6)} %select_n.123, s32[]{:T(128)S(6)} %select_n.124) | dynamic-update-slice | bytes 1048580 | tf_op jit(solution)/shard_map/dynamic_update_slice | solution.py:81
  99.8 8.4 %dynamic_update_slice.64 = f32[2,512,512]{2,1,0:T(8,128)S(1)} dynamic-update-slice(f32[2,512,512]{2,1,0:T(8,128)S(1)} %dynamic_update_slice.63, f32[2,256,256]{2,1,0:T(8,128)} %maximum_add_fusion, s32[]{:T(128)} %constant.14.clone.1, s32[]{:T(128)S(6)} %select_n.125, s32[]{:T(128)S(6)} %select_n.126) | dynamic-update-slice | bytes 1048580 | tf_op jit(solution)/shard_map/dynamic_update_slice | solution.py:81
  110.2 8.9 %dynamic_update_slice.65 = f32[2,512,512]{2,1,0:T(8,128)S(1)} dynamic-update-slice(f32[2,512,512]{2,1,0:T(8,128)S(1)} %dynamic_update_slice.64, f32[2,256,256]{2,1,0:T(8,128)} %maximum_add_fusion.1, s32[]{:T(128)} %constant.14.clone.1, s32[]{:T(128)S(6)} %select_n.127, s32[]{:T(128)S(6)} %select_n.128) | dynamic-update-slice | bytes 1048580 | tf_op jit(solution)/shard_map/dynamic_update_slice | solution.py:81
  120.0 9.1 %collective-permute-start.4 = (f32[2,512,128]{2,1,0:T(8,128)}, f32[2,512,128]{2,1,0:T(8,128)}, u32[]{:S(2)}, u32[]{:S(2)}) collective-permute-start(f32[2,512,128]{2,1,0:T(8,128)} %slice.282), channel_id=1, source_target_pairs={{1,0},{2,1},{3,2},{4,3},{5,4},{6,5},{7,6},{8,7},{9,8},{10,9},{11,1... | collective-permute-start | bytes 1572872 | tf_op jit(solution)/shard_map/ppermute | solution.py:20
  130.2 3.5 dynamic_update_slice.70
  134.9 3.8 dynamic_update_slice.71
  138.7 3.8 collective-permute-done.4
  147.5 3.9 dynamic_update_slice.72
  152.4 8.6 %collective-permute-start.8 = (f32[1,512,128]{2,1,0:T(8,128)S(1)}, f32[1,512,128]{2,1,0:T(8,128)S(1)}, u32[]{:S(2)}, u32[]{:S(2)}) collective-permute-start(f32[1,512,128]{2,1,0:T(8,128)S(1)} %slice.291), channel_id=1, source_target_pairs={{1,0},{2,1},{3,2},{4,3},{5,4},{6,5},{7,6},{8,7},{9,8},{10,9},{11,1... | collective-permute-start | bytes 786440 | tf_op jit(solution)/shard_map/ppermute | solution.py:20
  161.0 4.1 collective-permute-done.8
  172.1 13.8 %collective-permute-done.9 = f32[1,512,128]{2,1,0:T(8,128)S(1)} collective-permute-done((f32[1,512,128]{2,1,0:T(8,128)S(1)}, f32[1,512,128]{2,1,0:T(8,128)S(1)}, u32[]{:S(2)}, u32[]{:S(2)}) %collective-permute-start.9) | collective-permute-done | bytes 262176 | tf_op jit(solution)/shard_map/ppermute | solution.py:20
  187.9 3.9 collective-permute-done.10
  191.9 3.7 collective-permute-start.11
  202.4 100.2 %pmax.7 = f32[]{:T(128)} all-reduce(f32[]{:T(128)} %slice_reduce_fusion), channel_id=1, replica_groups=mesh['row'=16,'col'=32] {'row','col'}, use_global_device_ids=true, to_apply=%region_1.2 | all-reduce | flops 1 | bytes 8 | tf_op jit(solution)/shard_map/pmax | solution.py:109
  307.5 4.5 collective-permute-start.13
  318.5 8.1 %collective-permute-start.15 = (f32[2,512,128]{2,1,0:T(8,128)S(1)}, f32[2,512,128]{2,1,0:T(8,128)S(1)}, u32[]{:S(2)}, u32[]{:S(2)}) collective-permute-start(f32[2,512,128]{2,1,0:T(8,128)S(1)} %get-tuple-element.24), channel_id=1, source_target_pairs={{1,0},{2,1},{3,2},{4,3},{5,4},{6,5},{7,6},{8,7},{9,8},{10,9},{11,1... | collective-permute-start | bytes 1572872 | tf_op jit(solution)/shard_map/ppermute | solution.py:33
  326.6 9.9 %collective-permute-done.14 = f32[2,512,128]{2,1,0:T(8,128)S(1)} collective-permute-done((f32[2,512,128]{2,1,0:T(8,128)S(1)}, f32[2,512,128]{2,1,0:T(8,128)S(1)}, u32[]{:S(2)}, u32[]{:S(2)}) %collective-permute-start.14) | collective-permute-done | bytes 524320 | tf_op jit(solution)/shard_map/ppermute | solution.py:31
  336.5 11.0 %collective-permute-done.15 = f32[2,512,128]{2,1,0:T(8,128)S(1)} collective-permute-done((f32[2,512,128]{2,1,0:T(8,128)S(1)}, f32[2,512,128]{2,1,0:T(8,128)S(1)}, u32[]{:S(2)}, u32[]{:S(2)}) %collective-permute-start.15) | collective-permute-done | bytes 524320 | tf_op jit(solution)/shard_map/ppermute | solution.py:33
  389.0 8.0 %dynamic_update_slice.77 = f32[2,512,512]{2,1,0:T(8,128)S(1)} dynamic-update-slice(f32[2,512,512]{2,1,0:T(8,128)S(1)} %broadcast.23, f32[2,256,256]{2,1,0:T(8,128)S(1)} %pad_maximum_fusion.6, s32[]{:T(128)} %constant.14.clone.1, s32[]{:T(128)S(6)} %select_n.123, s32[]{:T(128)S(6)} %select_n.124) | dynamic-update-slice | bytes 1048580 | tf_op jit(solution)/shard_map/dynamic_update_slice | solution.py:81
  398.2 9.0 %dynamic_update_slice.78 = f32[2,512,512]{2,1,0:T(8,128)S(1)} dynamic-update-slice(f32[2,512,512]{2,1,0:T(8,128)S(1)} %dynamic_update_slice.77, f32[2,256,256]{2,1,0:T(8,128)S(1)} %maximum_add_fusion.2, s32[]{:T(128)} %constant.14.clone.1, s32[]{:T(128)S(6)} %select_n.125, s32[]{:T(128)S(6)} %select_n.126) | dynamic-update-slice | bytes 1048580 | tf_op jit(solution)/shard_map/dynamic_update_slice | solution.py:81
  408.5 9.9 %dynamic_update_slice.79 = f32[2,512,512]{2,1,0:T(8,128)S(1)} dynamic-update-slice(f32[2,512,512]{2,1,0:T(8,128)S(1)} %dynamic_update_slice.78, f32[2,256,256]{2,1,0:T(8,128)S(1)} %maximum_add_fusion.3, s32[]{:T(128)} %constant.14.clone.1, s32[]{:T(128)S(6)} %select_n.127, s32[]{:T(128)S(6)} %select_n.128) | dynamic-update-slice | bytes 1048580 | tf_op jit(solution)/shard_map/dynamic_update_slice | solution.py:81
  418.5 9.1 %collective-permute-start.16 = (f32[2,512,128]{2,1,0:T(8,128)S(1)}, f32[2,512,128]{2,1,0:T(8,128)S(1)}, u32[]{:S(2)}, u32[]{:S(2)}) collective-permute-start(f32[2,512,128]{2,1,0:T(8,128)S(1)} %slice.313), channel_id=1, source_target_pairs={{1,0},{2,1},{3,2},{4,3},{5,4},{6,5},{7,6},{8,7},{9,8},{10,9},{11,1... | collective-permute-start | bytes 1572872 | tf_op jit(solution)/shard_map/ppermute | solution.py:20
  427.5 11.1 %collective-permute-done.16 = f32[2,512,128]{2,1,0:T(8,128)S(1)} collective-permute-done((f32[2,512,128]{2,1,0:T(8,128)S(1)}, f32[2,512,128]{2,1,0:T(8,128)S(1)}, u32[]{:S(2)}, u32[]{:S(2)}) %collective-permute-start.16) | collective-permute-done | bytes 524320 | tf_op jit(solution)/shard_map/ppermute | solution.py:20
  440.7 14.3 %collective-permute-done.17 = f32[2,512,128]{2,1,0:T(8,128)S(1)} collective-permute-done((f32[2,512,128]{2,1,0:T(8,128)S(1)}, f32[2,512,128]{2,1,0:T(8,128)S(1)}, u32[]{:S(2)}, u32[]{:S(2)}) %collective-permute-start.17) | collective-permute-done | bytes 524320 | tf_op jit(solution)/shard_map/ppermute | solution.py:20
  455.3 23.3 %collective-permute-start.18 = (f32[2,128,512]{2,1,0:T(8,128)S(1)}, f32[2,128,512]{2,1,0:T(8,128)S(1)}, u32[]{:S(2)}, u32[]{:S(2)}) collective-permute-start(f32[2,128,512]{2,1,0:T(8,128)S(1)} %slice.317), channel_id=1, source_target_pairs={{32,0},{64,32},{96,64},{128,96},{160,128},{192,160},{224,192},{256... | collective-permute-start | bytes 1572872 | tf_op jit(solution)/shard_map/ppermute | solution.py:20
  478.5 12.1 %collective-permute-done.18 = f32[2,128,512]{2,1,0:T(8,128)S(1)} collective-permute-done((f32[2,128,512]{2,1,0:T(8,128)S(1)}, f32[2,128,512]{2,1,0:T(8,128)S(1)}, u32[]{:S(2)}, u32[]{:S(2)}) %collective-permute-start.18) | collective-permute-done | bytes 524320 | tf_op jit(solution)/shard_map/ppermute | solution.py:20
  492.8 9.6 %collective-permute-done.19 = f32[2,128,512]{2,1,0:T(8,128)S(1)} collective-permute-done((f32[2,128,512]{2,1,0:T(8,128)S(1)}, f32[2,128,512]{2,1,0:T(8,128)S(1)}, u32[]{:S(2)}, u32[]{:S(2)}) %collective-permute-start.19) | collective-permute-done | bytes 524320 | tf_op jit(solution)/shard_map/ppermute | solution.py:20
  (125 shorter events, 136.0 us)
Async XLA Ops:
  1.1 9.2 %collective-permute-start = (f32[2,128,256]{2,1,0:T(8,128)S(1)}, f32[2,128,256]{2,1,0:T(8,128)S(1)}, u32[]{:S(2)}, u32[]{:S(2)}) collective-permute-start(f32[2,128,256]{2,1,0:T(8,128)S(1)} %get-tuple-element.49), channel_id=1, source_target_pairs={{0,32},{32,64},{64,96},{96,128},{128,160},{160,192},{192,224},{224... | collective-permute-start | bytes 786440 | tf_op jit(solution)/shard_map/ppermute | solution.py:31
  3.0 21.3 %copy-start.10 = (s32[1,1,3,2]{2,3,1,0:T(2,128)S(1)}, s32[1,1,3,2]{2,3,1,0:T(2,128)}, u32[]{:S(2)}) copy-start(s32[1,1,3,2]{2,3,1,0:T(2,128)} %param.6) | copy-start | bytes 76
  3.0 33.4 %copy-start.9 = (f32[2,256,256]{2,1,0:T(8,128)S(1)}, f32[2,256,256]{2,1,0:T(8,128)}, u32[]{:S(2)}) copy-start(f32[2,256,256]{2,1,0:T(8,128)} %param.5) | copy-start | bytes 1572868
  3.0 8.5 %collective-permute-start.1 = (f32[2,128,256]{2,1,0:T(8,128)S(1)}, f32[2,128,256]{2,1,0:T(8,128)S(1)}, u32[]{:S(2)}, u32[]{:S(2)}) collective-permute-start(f32[2,128,256]{2,1,0:T(8,128)S(1)} %get-tuple-element.48), channel_id=1, source_target_pairs={{32,0},{64,32},{96,64},{128,96},{160,128},{192,160},{224,192},{256... | collective-permute-start | bytes 786440 | tf_op jit(solution)/shard_map/ppermute | solution.py:33
  11.7 24.8 %collective-permute-start.2 = (f32[2,512,128]{2,1,0:T(8,128)S(1)}, f32[2,512,128]{2,1,0:T(8,128)}, u32[]{:S(2)}, u32[]{:S(2)}) collective-permute-start(f32[2,512,128]{2,1,0:T(8,128)S(1)} %get-tuple-element.29), channel_id=1, source_target_pairs={{0,1},{1,2},{2,3},{3,4},{4,5},{5,6},{6,7},{7,8},{8,9},{9,10},{10,1... | collective-permute-start | bytes 1572872 | tf_op jit(solution)/shard_map/ppermute | solution.py:31
  16.0 31.9 %collective-permute-start.3 = (f32[2,512,128]{2,1,0:T(8,128)S(1)}, f32[2,512,128]{2,1,0:T(8,128)}, u32[]{:S(2)}, u32[]{:S(2)}) collective-permute-start(f32[2,512,128]{2,1,0:T(8,128)S(1)} %get-tuple-element.30), channel_id=1, source_target_pairs={{1,0},{2,1},{3,2},{4,3},{5,4},{6,5},{7,6},{8,7},{9,8},{10,9},{11,1... | collective-permute-start | bytes 1572872 | tf_op jit(solution)/shard_map/ppermute | solution.py:33
  36.4 49.4 %copy-start.3 = (f32[256,256]{1,0:T(8,128)}, f32[256,256]{1,0:T(8,128)S(1)}, u32[]{:S(2)}) copy-start(f32[256,256]{1,0:T(8,128)S(1)} %get-tuple-element.46) | copy-start | bytes 786436
  36.5 49.4 %copy-start.5 = (f32[256,256]{1,0:T(8,128)}, f32[256,256]{1,0:T(8,128)S(1)}, u32[]{:S(2)}) copy-start(f32[256,256]{1,0:T(8,128)S(1)} %get-tuple-element.47) | copy-start | bytes 786436
  64.3 4.6 copy-start
  120.0 22.5 %collective-permute-start.4 = (f32[2,512,128]{2,1,0:T(8,128)}, f32[2,512,128]{2,1,0:T(8,128)}, u32[]{:S(2)}, u32[]{:S(2)}) collective-permute-start(f32[2,512,128]{2,1,0:T(8,128)} %slice.282), channel_id=1, source_target_pairs={{1,0},{2,1},{3,2},{4,3},{5,4},{6,5},{7,6},{8,7},{9,8},{10,9},{11,1... | collective-permute-start | bytes 1572872 | tf_op jit(solution)/shard_map/ppermute | solution.py:20
  144.4 24.6 %collective-permute-start.5 = (f32[2,512,128]{2,1,0:T(8,128)}, f32[2,512,128]{2,1,0:T(8,128)}, u32[]{:S(2)}, u32[]{:S(2)}) collective-permute-start(f32[2,512,128]{2,1,0:T(8,128)} %get-tuple-element.16), channel_id=1, source_target_pairs={{0,1},{1,2},{2,3},{3,4},{4,5},{5,6},{6,7},{7,8},{8,9},{9,10},{10,1... | collective-permute-start | bytes 1572872 | tf_op jit(solution)/shard_map/ppermute | solution.py:20
  152.4 12.7 %collective-permute-start.8 = (f32[1,512,128]{2,1,0:T(8,128)S(1)}, f32[1,512,128]{2,1,0:T(8,128)S(1)}, u32[]{:S(2)}, u32[]{:S(2)}) collective-permute-start(f32[1,512,128]{2,1,0:T(8,128)S(1)} %slice.291), channel_id=1, source_target_pairs={{1,0},{2,1},{3,2},{4,3},{5,4},{6,5},{7,6},{8,7},{9,8},{10,9},{11,1... | collective-permute-start | bytes 786440 | tf_op jit(solution)/shard_map/ppermute | solution.py:20
  166.9 19.0 %copy-start.1 = (f32[1,512,512]{2,1,0:T(8,128)S(1)}, f32[1,512,512]{2,1,0:T(8,128)}, u32[]{:S(2)}) copy-start(f32[1,512,512]{2,1,0:T(8,128)} %get-tuple-element.28) | copy-start | bytes 3145732
  166.9 19.0 %collective-permute-start.9 = (f32[1,512,128]{2,1,0:T(8,128)S(1)}, f32[1,512,128]{2,1,0:T(8,128)S(1)}, u32[]{:S(2)}, u32[]{:S(2)}) collective-permute-start(f32[1,512,128]{2,1,0:T(8,128)S(1)} %get-tuple-element.27), channel_id=1, source_target_pairs={{0,1},{1,2},{2,3},{3,4},{4,5},{5,6},{6,7},{7,8},{8,9},{9,10},{10,1... | collective-permute-start | bytes 786440 | tf_op jit(solution)/shard_map/ppermute | solution.py:20
  170.2 25.4 %collective-permute-start.6 = (f32[2,128,512]{2,1,0:T(8,128)S(1)}, f32[2,128,512]{2,1,0:T(8,128)S(1)}, u32[]{:S(2)}, u32[]{:S(2)}) collective-permute-start(f32[2,128,512]{2,1,0:T(8,128)S(1)} %slice.286), channel_id=1, source_target_pairs={{32,0},{64,32},{96,64},{128,96},{160,128},{192,160},{224,192},{256... | collective-permute-start | bytes 1572872 | tf_op jit(solution)/shard_map/ppermute | solution.py:20
  186.0 5.8 %collective-permute-start.10 = (f32[1,128,512]{2,1,0:T(8,128)S(1)}, f32[1,128,512]{2,1,0:T(8,128)S(1)}, u32[]{:S(2)}, u32[]{:S(2)}) collective-permute-start(f32[1,128,512]{2,1,0:T(8,128)S(1)} %slice.295), channel_id=1, source_target_pairs={{32,0},{64,32},{96,64},{128,96},{160,128},{192,160},{224,192},{256... | collective-permute-start | bytes 786440 | tf_op jit(solution)/shard_map/ppermute | solution.py:20
  191.9 8.8 %collective-permute-start.11 = (f32[1,128,512]{2,1,0:T(8,128)S(1)}, f32[1,128,512]{2,1,0:T(8,128)S(1)}, u32[]{:S(2)}, u32[]{:S(2)}) collective-permute-start(f32[1,128,512]{2,1,0:T(8,128)S(1)} %get-tuple-element.25), channel_id=1, source_target_pairs={{0,32},{32,64},{64,96},{96,128},{128,160},{160,192},{192,224},{224... | collective-permute-start | bytes 786440 | tf_op jit(solution)/shard_map/ppermute | solution.py:20
  196.7 107.6 %collective-permute-start.7 = (f32[2,128,512]{2,1,0:T(8,128)}, f32[2,128,512]{2,1,0:T(8,128)S(1)}, u32[]{:S(2)}, u32[]{:S(2)}) collective-permute-start(f32[2,128,512]{2,1,0:T(8,128)} %get-tuple-element.14), channel_id=1, source_target_pairs={{0,32},{32,64},{64,96},{96,128},{128,160},{160,192},{192,224},{224... | collective-permute-start | bytes 1572872 | tf_op jit(solution)/shard_map/ppermute | solution.py:20
  200.7 1.0 copy-start.2
  304.3 1.3 copy-start.7
  305.6 8.6 %collective-permute-start.12 = (f32[2,128,256]{2,1,0:T(8,128)S(1)}, f32[2,128,256]{2,1,0:T(8,128)S(1)}, u32[]{:S(2)}, u32[]{:S(2)}) collective-permute-start(f32[2,128,256]{2,1,0:T(8,128)S(1)} %get-tuple-element.43), channel_id=1, source_target_pairs={{0,32},{32,64},{64,96},{96,128},{128,160},{160,192},{192,224},{224... | collective-permute-start | bytes 786440 | tf_op jit(solution)/shard_map/ppermute | solution.py:31
  307.5 8.4 %collective-permute-start.13 = (f32[2,128,256]{2,1,0:T(8,128)S(1)}, f32[2,128,256]{2,1,0:T(8,128)S(1)}, u32[]{:S(2)}, u32[]{:S(2)}) collective-permute-start(f32[2,128,256]{2,1,0:T(8,128)S(1)} %get-tuple-element.44), channel_id=1, source_target_pairs={{32,0},{64,32},{96,64},{128,96},{160,128},{192,160},{224,192},{256... | collective-permute-start | bytes 786440 | tf_op jit(solution)/shard_map/ppermute | solution.py:33
  316.1 20.4 %collective-permute-start.14 = (f32[2,512,128]{2,1,0:T(8,128)S(1)}, f32[2,512,128]{2,1,0:T(8,128)S(1)}, u32[]{:S(2)}, u32[]{:S(2)}) collective-permute-start(f32[2,512,128]{2,1,0:T(8,128)S(1)} %get-tuple-element.23), channel_id=1, source_target_pairs={{0,1},{1,2},{2,3},{3,4},{4,5},{5,6},{6,7},{7,8},{8,9},{9,10},{10,1... | collective-permute-start | bytes 1572872 | tf_op jit(solution)/shard_map/ppermute | solution.py:31
  318.5 29.0 %collective-permute-start.15 = (f32[2,512,128]{2,1,0:T(8,128)S(1)}, f32[2,512,128]{2,1,0:T(8,128)S(1)}, u32[]{:S(2)}, u32[]{:S(2)}) collective-permute-start(f32[2,512,128]{2,1,0:T(8,128)S(1)} %get-tuple-element.24), channel_id=1, source_target_pairs={{1,0},{2,1},{3,2},{4,3},{5,4},{6,5},{7,6},{8,7},{9,8},{10,9},{11,1... | collective-permute-start | bytes 1572872 | tf_op jit(solution)/shard_map/ppermute | solution.py:33
  348.2 1.0 copy-start.4
  348.2 1.0 copy-start.6
  418.5 20.2 %collective-permute-start.16 = (f32[2,512,128]{2,1,0:T(8,128)S(1)}, f32[2,512,128]{2,1,0:T(8,128)S(1)}, u32[]{:S(2)}, u32[]{:S(2)}) collective-permute-start(f32[2,512,128]{2,1,0:T(8,128)S(1)} %slice.313), channel_id=1, source_target_pairs={{1,0},{2,1},{3,2},{4,3},{5,4},{6,5},{7,6},{8,7},{9,8},{10,9},{11,1... | collective-permute-start | bytes 1572872 | tf_op jit(solution)/shard_map/ppermute | solution.py:20
  438.8 16.3 %collective-permute-start.17 = (f32[2,512,128]{2,1,0:T(8,128)S(1)}, f32[2,512,128]{2,1,0:T(8,128)S(1)}, u32[]{:S(2)}, u32[]{:S(2)}) collective-permute-start(f32[2,512,128]{2,1,0:T(8,128)S(1)} %get-tuple-element.7), channel_id=1, source_target_pairs={{0,1},{1,2},{2,3},{3,4},{4,5},{5,6},{6,7},{7,8},{8,9},{9,10},{10,1... | collective-permute-start | bytes 1572872 | tf_op jit(solution)/shard_map/ppermute | solution.py:20
  455.2 47.3 %copy-start.8 = (f32[256,256]{1,0:T(8,128)S(1)}, f32[256,256]{1,0:T(8,128)}, u32[]{:S(2)}) copy-start(f32[256,256]{1,0:T(8,128)} %copy-done.7) | copy-start | bytes 786436
  455.3 35.4 %collective-permute-start.18 = (f32[2,128,512]{2,1,0:T(8,128)S(1)}, f32[2,128,512]{2,1,0:T(8,128)S(1)}, u32[]{:S(2)}, u32[]{:S(2)}) collective-permute-start(f32[2,128,512]{2,1,0:T(8,128)S(1)} %slice.317), channel_id=1, source_target_pairs={{32,0},{64,32},{96,64},{128,96},{160,128},{192,160},{224,192},{256... | collective-permute-start | bytes 1572872 | tf_op jit(solution)/shard_map/ppermute | solution.py:20
  490.9 11.6 %collective-permute-start.19 = (f32[2,128,512]{2,1,0:T(8,128)S(1)}, f32[2,128,512]{2,1,0:T(8,128)S(1)}, u32[]{:S(2)}, u32[]{:S(2)}) collective-permute-start(f32[2,128,512]{2,1,0:T(8,128)S(1)} %get-tuple-element.5), channel_id=1, source_target_pairs={{0,32},{32,64},{64,96},{96,128},{128,160},{160,192},{192,224},{224... | collective-permute-start | bytes 1572872 | tf_op jit(solution)/shard_map/ppermute | solution.py:20
where the time goes:
time: 512 us; the launch traced here: 504 us
  waiting for transfers between devices  114 us (22%)
  starting transfers between devices  103 us (20%)
  blocking collectives  100 us (20%)
  matrix products  75.9 us (15%)
  local copies, waits for them, and re-layouts  75.1 us (15%)
  other arithmetic  22.2 us (4%)
  between operations  13.3 us (3%)
    pmax x1, blocking collectives, owned_peak(): return lax.pmax(local_peak, ('row', 'col'))  100 us
    ppermute x12, waiting for transfers between devices, from_behind(): return lax.ppermute(block, axis, route)  74.8 us
    ppermute x12, starting transfers between devices, from_behind(): return lax.ppermute(block, axis, route)  67.3 us
    dynamic_update_slice x9, local copies, waits for them, and re-layouts, add_window(): lax.dynamic_update_slice(total, block + piece, (zero_index, top, left))  63 us
    dot_general x16, matrix products, mat_left(): jnp.einsum('kn,pnm->pkm', matrix, stacked, precision=lax.Precision.HIGHEST)  39.2 us
    dot_general x16, matrix products, mat_right(): jnp.einsum('pnm,mk->pnk', stacked, matrix, precision=lax.Precision.HIGHEST)  36.7 us
    ppermute x4, starting transfers between devices, padded(): lax.ppermute(head, axis, [((i + 1) % count, i) for i in range(ends)])  25.7 us
    ppermute x4, waiting for transfers between devices, padded(): lax.ppermute(head, axis, [((i + 1) % count, i) for i in range(ends)])  24.4 us
  transfers between devices with their start and end apart: 20, of which 16 were waited for; matrix products, arithmetic and copies ran while one was open for 5% of the time, Pallas kernels for 0%

commit v1 on v0

v1 whole, which is shorter than its diff:
```python
import functools
import math

import jax
import jax.numpy as jnp
import ml_dtypes
import numpy as np
from jax import lax
from jax.experimental import pallas as pl
from jax.experimental.pallas import tpu as pltpu
from jax.sharding import PartitionSpec as P

WIN = 256
HALF = 128
HALO = 128
ITERS = 2
SMOOTH = 0.25
RIDGE = 0.1
MESH = pl.DeviceIdType.MESH

NEIGHBOURS = [(a, b) for a in (-1, 0, 1) for b in (-1, 0, 1) if (a, b) != (0, 0)]


def dft_tables():
    n = np.arange(HALF)[None, :]
    m = np.arange(HALF)[:, None]
    blocks = []
    for freq in (2 * m, 2 * m + 1):
        angle = -2.0 * math.pi * ((freq * n) % WIN) / WIN
        re, im = np.cos(angle) / 16.0, np.sin(angle) / 16.0
        blocks.append(np.block([[re, -im], [im, re]]))
    out = []
    for block in (blocks[0], blocks[1], blocks[0].T, blocks[1].T):
        high = block.astype(ml_dtypes.bfloat16)
        low = (block - high.astype(np.float64)).astype(ml_dtypes.bfloat16)
        out += [high, low]
    order = np.concatenate([np.arange(0, WIN, 2), np.arange(1, WIN, 2)])
    perm = (order[:, None] == np.arange(WIN)[None, :]).astype(ml_dtypes.bfloat16)
    out += [perm, perm.T]
    return np.stack(out)


def split(x):
    high = x.astype(jnp.bfloat16)
    low = (x - high.astype(jnp.float32)).astype(jnp.bfloat16)
    return high, low


def dot(a, b):
    return jnp.dot(a, b, preferred_element_type=jnp.float32)


def left(tab, index, x):
    high, low = split(x)
    th, tl = tab[2 * index], tab[2 * index + 1]
    return dot(jnp.concatenate([th, th, tl], axis=1), jnp.concatenate([high, low, high], axis=0))


def right(x, tab, index):
    high, low = split(x)
    th, tl = tab[2 * index], tab[2 * index + 1]
    return dot(jnp.concatenate([high, low, high], axis=1), jnp.concatenate([th, th, tl], axis=0))


def digits(size, part):
    return (size // part, part) if size > part else (1, size)


def kernel(
    n_row, n_col, n_pos,
    spec, probe_in, off, amp_in, tab_in,
    out,
    span_a, span_b, grad, wide, pad, light, inv, probe, amp, tab, noff, row_in, col_in, peak_out, peak_in,
    local_sem, off_sem, span_send, span_recv, fold_send, fold_recv, peak_send, peak_recv,
):
    r, c = lax.axis_index("row"), lax.axis_index("col")
    f32 = jnp.float32
    spans = (span_a, span_b)
    lane = lax.broadcasted_iota(jnp.int32, (1, HALF), 1)

    def exists(dr, dc):
        ok = None
        for index, step, size in ((r, dr, n_row), (c, dc, n_col)):
            if step:
                here = (index + step >= 0) & (index + step < size)
                ok = here if ok is None else ok & here
        return ok

    ra, rb = digits(n_row, 4)
    ca, cb = digits(n_col, 8)
    groups = []
    for phase, (size, place) in enumerate(
        (
            (rb, lambda j: {"row": (r // rb) * rb + (r % rb + j) % rb, "col": c}),
            (cb, lambda j: {"row": r, "col": (c // cb) * cb + (c % cb + j) % cb}),
            (ra, lambda j: {"row": ((r // rb + j) % ra) * rb + r % rb, "col": c}),
            (ca, lambda j: {"row": r, "col": ((c // cb + j) % ca) * cb + c % cb}),
        )
    ):
        groups.append([(j, place(j)) for j in range(1, size)])

    for k in range(9):
        for p in range(n_pos):
            for d in range(2):
                if k == 4:
                    noff[k, p, d] = off[0, 0, p, d]
                else:
                    noff[k, p, d] = 4096

    for k in range(2):
        for dr, dc, place in (
            (-1, 0, (slice(None), pl.ds(0, HALO))),
            (1, 0, (slice(None), pl.ds(HALO + WIN, HALO))),
            (0, -1, (0, pl.ds(HALO, WIN))),
            (0, 1, (3, pl.ds(HALO, WIN))),
        ):
            @pl.when(jnp.logical_not(exists(dr, dc)))
            def _(k=k, place=place):
                ref = spans[k].at[(slice(None),) + place + (slice(None),)]
                ref[...] = jnp.zeros(ref.shape, f32)

    barrier = pltpu.get_barrier_semaphore()
    total = 0
    for dr, dc in NEIGHBOURS:
        here = exists(dr, dc)
        total = total + here.astype(jnp.int32)

        @pl.when(here)
        def _(dr=dr, dc=dc):
            pl.semaphore_signal(barrier, inc=1, device_id={"row": r + dr, "col": c + dc}, device_id_type=MESH)

    for group in groups:
        for j, place in group:
            pl.semaphore_signal(barrier, inc=1, device_id=place, device_id_type=MESH)
            total = total + 1

    copies = [
        pltpu.make_async_copy(spec.at[:, :, pl.ds(0, HALF)], span_a.at[:, 1, pl.ds(HALO, WIN), :], local_sem.at[0]),
        pltpu.make_async_copy(spec.at[:, :, pl.ds(HALF, HALF)], span_a.at[:, 2, pl.ds(HALO, WIN), :], local_sem.at[1]),
        pltpu.make_async_copy(probe_in, probe, local_sem.at[2]),
        pltpu.make_async_copy(tab_in, tab, local_sem.at[3]),
        pltpu.make_async_copy(amp_in.at[0, 0], amp, local_sem.at[4]),
    ]
    for copy in copies:
        copy.start()

    pl.semaphore_wait(barrier, total)

    def remote(src, dst, send, recv, dr, dc):
        return pltpu.make_async_remote_copy(
            src, dst, send, recv, device_id={"row": r + dr, "col": c + dc}, device_id_type=MESH
        )

    def start(copy, dr, dc):
        @pl.when(exists(dr, dc))
        def _():
            copy.start()

    def finish(copy, dr, dc):
        @pl.when(exists(dr, dc))
        def _():
            copy.wait_send()

        @pl.when(exists(-dr, -dc))
        def _():
            copy.wait_recv()

    def widen_col(k):
        out_copies = []
        for i, (dc, tile, there) in enumerate(((-1, 1, 3), (1, 2, 0))):
            if k == 0:
                src = spec.at[:, :, pl.ds((tile - 1) * HALF, HALF)]
            else:
                src = spans[k].at[:, tile, pl.ds(HALO, WIN), :]
            dst = spans[k].at[:, there, pl.ds(HALO, WIN), :]
            copy = remote(src, dst, span_send.at[k, i], span_recv.at[k, i], 0, dc)
            start(copy, 0, dc)
            out_copies.append((copy, 0, dc))
        return out_copies

    def widen_row(k):
        out_copies = []
        for i, (dr, here, there) in enumerate(((-1, HALO, HALO + WIN), (1, WIN, 0))):
            src = spans[k].at[:, :, pl.ds(here, HALO), :]
            dst = spans[k].at[:, :, pl.ds(there, HALO), :]
            copy = remote(src, dst, span_send.at[k, 2 + i], span_recv.at[k, 2 + i], dr, 0)
            start(copy, dr, 0)
            out_copies.append((copy, dr, 0))
        return out_copies

    first = widen_col(0)
    off_copies = []
    for i, (dr, dc) in enumerate(NEIGHBOURS):
        slot = (-dr + 1) * 3 + (-dc + 1)
        copy = remote(off.at[0, 0], noff.at[slot], off_sem.at[0, i], off_sem.at[1, i], dr, dc)
        start(copy, dr, dc)
        off_copies.append((copy, dr, dc))

    def clear(ref, count):
        def body(i, _):
            ref[i] = jnp.zeros(ref.shape[1:], f32)
            return 0

        lax.fori_loop(0, count, body, 0)

    clear(pad, 7)
    copies[2].wait()
    copies[0].wait()
    copies[1].wait()
    for t in range(2):
        cols = pl.ds(t * HALF, HALF)
        pad[2 + t, pl.ds(WIN, WIN), :] = probe[0, :, cols] * probe[0, :, cols] + probe[1, :, cols] * probe[1, :, cols]

    def clear_wide(i, _):
        p, rest = i // 12, i % 12
        wide[p, rest // 6, rest % 6] = jnp.zeros((3 * WIN, HALF), f32)
        return 0

    lax.fori_loop(0, n_pos * 12, clear_wide, 0)

    for item in first:
        finish(*item)
    second = widen_row(0)

    for item in off_copies:
        finish(*item)

    light[...] = jnp.zeros(light.shape, f32)

    def add_light(i, _):
        near, p = i // n_pos, i % n_pos
        top = jnp.clip(noff[near, p, 0] + (near // 3 - 1) * WIN, -WIN, WIN)
        side = jnp.clip(noff[near, p, 1] + (near % 3 - 1) * WIN, -WIN, WIN)
        rows = pl.ds(WIN - top, WIN)
        start_col = WIN - side
        q, s = start_col // HALF, start_col % HALF
        turn = (HALF - s) % HALF
        rolled = [pltpu.roll(pad[q + j, rows, :], turn, 1) for j in range(3)]
        keep = lane < HALF - s
        for t in range(2):
            light[t] = light[t] + jnp.where(keep, rolled[t], rolled[t + 1])
        return 0

    lax.fori_loop(0, 9 * n_pos, add_light, 0)

    peak = jnp.max(light[...].reshape(2 * WIN // 8, 8, HALF), axis=0)

    def peak_start(phase, value):
        peak_out[phase] = value
        items = []
        for j, place in groups[phase]:
            copy = pltpu.make_async_remote_copy(
                peak_out.at[phase], peak_in.at[phase, j], peak_send.at[phase, j], peak_recv.at[phase, j],
                device_id=place, device_id_type=MESH,
            )
            copy.start()
            items.append(copy)
        return items

    def peak_finish(phase, items):
        for copy in items:
            copy.wait()
        value = peak_out[phase]
        for j, _ in groups[phase]:
            value = jnp.maximum(value, peak_in[phase, j])
        return value

    items = peak_start(0, peak)

    copies[3].wait()
    copies[4].wait()

    def order_amp(p, _):
        rows = tab[8]
        high, low = split(amp[p])
        x = dot(jnp.concatenate([rows, rows], axis=1), jnp.concatenate([high, low], axis=0))
        high, low = split(x)
        cols = tab[9]
        amp[p] = dot(jnp.concatenate([high, low], axis=1), jnp.concatenate([cols, cols], axis=0))
        return 0

    lax.fori_loop(0, n_pos, order_amp, 0)
    peak = peak_finish(0, items)
    items = peak_start(1, peak)

    for item in second:
        finish(*item)

    def cat(a, b, axis):
        return jnp.concatenate([a, b], axis=axis)

    def window(k, p):
        top = off[0, 0, p, 0] + HALO
        side = off[0, 0, p, 1] + HALO
        q, s = side // HALF, side % HALF
        rows = pl.ds(top, WIN)
        turn = (HALF - s) % HALF
        keep = lane < HALF - s
        patch = []
        for part in range(2):
            rolled = [
                pltpu.roll(spans[k][part, jnp.minimum(q + j, 3), rows, :], turn, 1) for j in range(3)
            ]
            patch.append(cat(jnp.where(keep, rolled[0], rolled[1]), jnp.where(keep, rolled[1], rolled[2]), 1))
        pr, pi = probe[0], probe[1]
        er = pr * patch[0] - pi * patch[1]
        ei = pr * patch[1] + pi * patch[0]
        sums = cat(er[:HALF] + er[HALF:], ei[:HALF] + ei[HALF:], 0)
        difs = cat(er[:HALF] - er[HALF:], ei[:HALF] - ei[HALF:], 0)
        even = left(tab, 0, sums)
        odd = left(tab, 1, difs)
        xr = cat(even[:HALF], odd[:HALF], 0)
        xi = cat(even[HALF:], odd[HALF:], 0)
        sums = cat(xr[:, :HALF] + xr[:, HALF:], xi[:, :HALF] + xi[:, HALF:], 1)
        difs = cat(xr[:, :HALF] - xr[:, HALF:], xi[:, :HALF] - xi[:, HALF:], 1)
        out_cols = []
        for index, x in ((0, sums), (1, difs)):
            far = right(x, tab, 2 + index)
            fr, fi = far[:, :HALF], far[:, HALF:]
            factor = 1.0 - amp[p, :, pl.ds(index * HALF, HALF)] * lax.rsqrt(fr * fr + fi * fi + SMOOTH)
            out_cols.append(right(cat(factor * fr, factor * fi, 1), tab, index))
        lo, hi = out_cols[0] + out_cols[1], out_cols[0] - out_cols[1]
        xr = cat(lo[:, :HALF], hi[:, :HALF], 1)
        xi = cat(lo[:, HALF:], hi[:, HALF:], 1)
        even = left(tab, 2, cat(xr[:HALF], xi[:HALF], 0))
        odd = left(tab, 3, cat(xr[HALF:], xi[HALF:], 0))
        lo, hi = even + odd, even - odd
        br = cat(lo[:HALF], hi[:HALF], 0)
        bi = cat(lo[HALF:], hi[HALF:], 0)
        g = (pr * br + pi * bi, pr * bi - pi * br)
        past = lane >= s
        zero = jnp.zeros((WIN, HALF), f32)
        for part in range(2):
            one = pltpu.roll(g[part][:, :HALF], s, 1)
            two = pltpu.roll(g[part][:, HALF:], s, 1)
            wide[p, part, 2, pl.ds(WIN, WIN), :] = jnp.where(past, one, zero)
            wide[p, part, 3, pl.ds(WIN, WIN), :] = jnp.where(past, two, one)
            wide[p, part, 4, pl.ds(WIN, WIN), :] = jnp.where(past, zero, two)

    def gather(k):
        def body(i, _):
            part, t = i // 4, i % 4
            for chunk in range(4):
                acc = None
                for p in range(n_pos):
                    top = off[0, 0, p, 0] + HALO
                    q = (off[0, 0, p, 1] + HALO) // HALF
                    piece = wide[p, part, 2 + t - q, pl.ds(WIN - top + chunk * HALF, HALF), :]
                    acc = piece if acc is None else acc + piece
                grad[k, part, t, pl.ds(chunk * HALF, HALF), :] = acc
            return 0

        lax.fori_loop(0, 8, body, 0)

    for k in range(ITERS):
        lax.fori_loop(0, n_pos, lambda p, _, k=k: (window(k, p), 0)[1], 0)
        gather(k)

        sent = []
        for i, (dr, here) in enumerate(((-1, 0), (1, HALO + WIN))):
            copy = remote(
                grad.at[k, :, :, pl.ds(here, HALO), :], row_in.at[k, i], fold_send.at[k, i], fold_recv.at[k, i], dr, 0
            )
            start(copy, dr, 0)
            sent.append((copy, dr, 0))
        if k == 0:
            peak = peak_finish(1, items)
            items = peak_start(2, peak)
        for i, (copy, dr, dc) in enumerate(sent):
            finish(copy, dr, dc)
            rows = pl.ds(WIN, HALO) if dr < 0 else pl.ds(HALO, HALO)

            @pl.when(exists(-dr, 0))
            def _(i=i, rows=rows):
                for part in range(2):
                    for t in range(4):
                        grad[k, part, t, rows, :] = grad[k, part, t, rows, :] + row_in[k, i, part, t]

        sent = []
        for i, (dc, here) in enumerate(((-1, 0), (1, 3))):
            copy = remote(
                grad.at[k, :, here, pl.ds(HALO, WIN), :], col_in.at[k, i],
                fold_send.at[k, 2 + i], fold_recv.at[k, 2 + i], 0, dc,
            )
            start(copy, 0, dc)
            sent.append((copy, 0, dc))
        if k == 0:
            peak = peak_finish(2, items)
            items = peak_start(3, peak)
            peak = jnp.max(peak_finish(3, items))
            inv[...] = 1.0 / (light[...] + RIDGE * peak)
        for i, (copy, dr, dc) in enumerate(sent):
            finish(copy, dr, dc)
            t = 2 if dc < 0 else 1

            @pl.when(exists(0, -dc))
            def _(i=i, t=t):
                for part in range(2):
                    grad[k, part, t, pl.ds(HALO, WIN), :] = grad[k, part, t, pl.ds(HALO, WIN), :] + col_in[k, i, part]

        for t in range(2):
            for part in range(2):
                new = spans[k][part, 1 + t, pl.ds(HALO, WIN), :] - grad[k, part, 1 + t, pl.ds(HALO, WIN), :] * inv[t]
                if k + 1 < ITERS:
                    spans[k + 1][part, 1 + t, pl.ds(HALO, WIN), :] = new
                else:
                    out[part, :, pl.ds(t * HALF, HALF)] = new
        if k + 1 < ITERS:
            for item in widen_col(k + 1):
                finish(*item)
            for item in widen_row(k + 1):
                finish(*item)


def solution(mesh):
    n_row, n_col = mesh.shape["row"], mesh.shape["col"]
    tables = dft_tables()

    def local(specimen, probe_field, offsets, amplitudes):
        n_pos = offsets.shape[2]
        vmem = lambda *shape: pltpu.VMEM(shape, jnp.float32)
        dma = lambda *shape: pltpu.SemaphoreType.DMA(shape)
        return pl.pallas_call(
            functools.partial(kernel, n_row, n_col, n_pos),
            out_shape=jax.ShapeDtypeStruct((2, WIN, WIN), jnp.float32),
            in_specs=[
                pl.BlockSpec(memory_space=pl.ANY),
                pl.BlockSpec(memory_space=pl.ANY),
                pl.BlockSpec(memory_space=pltpu.SMEM),
                pl.BlockSpec(memory_space=pl.ANY),
                pl.BlockSpec(memory_space=pl.ANY),
            ],
            out_specs=pl.BlockSpec(memory_space=pltpu.VMEM),
            scratch_shapes=[
                vmem(2, 4, 512, HALF),
                vmem(2, 4, 512, HALF),
                vmem(ITERS, 2, 4, 512, HALF),
                vmem(n_pos, 2, 6, 3 * WIN, HALF),
                vmem(7, 3 * WIN, HALF),
                vmem(2, WIN, HALF),
                vmem(2, WIN, HALF),
                vmem(2, WIN, WIN),
                vmem(n_pos, WIN, WIN),
                pltpu.VMEM((10, WIN, WIN), jnp.bfloat16),
                pltpu.SMEM((9, n_pos, 2), jnp.int32),
                vmem(ITERS, 2, 2, 4, HALO, HALF),
                vmem(ITERS, 2, 2, WIN, HALF),
                vmem(4, 8, HALF),
                vmem(4, 8, 8, HALF),
                dma(5),
                dma(2, 8),
                dma(ITERS, 4),
                dma(ITERS, 4),
                dma(ITERS, 4),
                dma(ITERS, 4),
                dma(4, 8),
                dma(4, 8),
            ],
            compiler_params=pltpu.CompilerParams(
                collective_id=0, has_side_effects=True, vmem_limit_bytes=56 * 1024 * 1024
            ),
        )(specimen, probe_field, offsets, amplitudes, jnp.asarray(tables))

    return jax.shard_map(
        local,
        mesh=mesh,
        in_specs=(
            P(None, "row", "col"),
            P(),
            P("row", "col", None, None),
            P("row", "col", None, None, None),
        ),
        out_specs=P(None, "row", "col"),
        check_vma=False,
    )
```

time: 512 us -> 136 us (0.27)
  the two profiles are of different devices: /device:TPU:36 before, /device:TPU:43 now
where the time goes in v1:
time: 136 us
  Pallas kernels  133 us (98%)
  local copies, waits for them, and re-layouts  3.2 us (2%)
    pallas_call x1, Pallas kernels, local(): pl.pallas_call(functools.partial(kernel, n_row, n_col, n_pos), out_shape=...  133 us
    unnamed x2, local copies, waits for them, and re-layouts  3.2 us

profile of v1, /device:TPU:43, one launch (start us, length us, event | category | flops | bytes accessed | tf_op | source)
XLA Modules:
  0.0 136.2 jit_solution(2215779144481848142)
XLA Ops:
  0.0 1.3 copy.6.off
  1.3 133.0 %shard_map.55 = f32[2,256,256]{2,1,0:T(8,128)} custom-call(f32[2,256,256]{2,1,0:T(8,128)} %spec.1, f32[2,256,256]{2,1,0:T(8,128)} %probe_in.1, s32[1,1,3,2]{3,2,1,0:T(4,128)} %copy.6.off, f32[1,1,3,256,256]{4,3,2,1,0:T(8,128)} %amp_in.1, bf16[10,256,256]{2,1,0:T(8,128)(2,1)} %constant.2.clone.tab_in), custom_call_target="tpu_custom_call" | custom-call | tf_op jit(solution)/shard_map/pallas_call | solution.py:423
  134.4 1.9 %copy.8 = f32[2,256,256]{2,1,0:T(8,128)} copy(f32[2,256,256]{2,1,0:T(8,128)} %shard_map.55) | data formatting | bytes 1048576

commit v2 on v1

--- a/solution.py
+++ b/solution.py
@@ -66,17 +66,58 @@
     return (size // part, part) if size > part else (1, size)
 
 
+Z_LEN = 8
+CHUNKS = 2
+
+
+class Message:
+    def __init__(self, pool, device, send_if, recv_if, src, dst):
+        send, recv, index = pool[0], pool[1], pool[2]
+        pool[2] += 1
+        self.send_if, self.recv_if = send_if, recv_if
+        self.copy = pltpu.make_async_remote_copy(
+            src, dst, send.at[index], recv.at[index], device_id=device, device_id_type=MESH
+        )
+
+    def _when(self, cond, action):
+        if cond is None:
+            action()
+        else:
+            pl.when(cond)(action)
+
+    def start(self):
+        self._when(self.send_if, self.copy.start)
+
+    def recv(self):
+        self._when(self.recv_if, self.copy.wait_recv)
+
+    def sent(self):
+        self._when(self.send_if, self.copy.wait_send)
+
+
 def kernel(
     n_row, n_col, n_pos,
     spec, probe_in, off, amp_in, tab_in,
     out,
-    span_a, span_b, grad, wide, pad, light, inv, probe, amp, tab, noff, row_in, col_in, peak_out, peak_in,
-    local_sem, off_sem, span_send, span_recv, fold_send, fold_recv, peak_send, peak_recv,
+    span_a, span_b, grad, wide, pad, light, inv, probe, amp, tab, noff,
+    corner_in, core_in, row_in, col_in, relay_strip, relay_corner, peak_out, peak_in,
+    local_sem, off_sem, send_sem, recv_sem, peak_send, peak_recv,
 ):
     r, c = lax.axis_index("row"), lax.axis_index("col")
     f32 = jnp.float32
     spans = (span_a, span_b)
     lane = lax.broadcasted_iota(jnp.int32, (1, HALF), 1)
+    pool = [send_sem, recv_sem, 0]
+
+    odd = r % 2
+    near = pl.multiple_of(HALO + HALF - HALF * odd, HALF)
+    far = pl.multiple_of(HALO + HALF * odd, HALF)
+    inner = pl.multiple_of((HALO + WIN) * (1 - odd), HALF)
+    outer = pl.multiple_of((HALO + WIN) * odd, HALF)
+    partner = {"row": r + 1 - 2 * odd, "col": c}
+    r_out = r - 1 + 2 * odd
+    has_outer = (r_out >= 0) & (r_out < n_row)
+    beyond = {"row": r_out, "col": c}
 
     def exists(dr, dc):
         ok = None
@@ -86,16 +127,17 @@
                 ok = here if ok is None else ok & here
         return ok
 
+    def col_ok(x):
+        return (x >= 0) & (x < n_col)
+
     ra, rb = digits(n_row, 4)
-    ca, cb = digits(n_col, 8)
+    ca, cb = digits(n_col, Z_LEN)
     groups = []
-    for phase, (size, place) in enumerate(
-        (
-            (rb, lambda j: {"row": (r // rb) * rb + (r % rb + j) % rb, "col": c}),
-            (cb, lambda j: {"row": r, "col": (c // cb) * cb + (c % cb + j) % cb}),
-            (ra, lambda j: {"row": ((r // rb + j) % ra) * rb + r % rb, "col": c}),
-            (ca, lambda j: {"row": r, "col": ((c // cb + j) % ca) * cb + c % cb}),
-        )
+    for size, place in (
+        (rb, lambda j: {"row": (r // rb) * rb + (r % rb + j) % rb, "col": c}),
+        (cb, lambda j: {"row": r, "col": (c // cb) * cb + (c % cb + j) % cb}),
+        (ra, lambda j: {"row": ((r // rb + j) % ra) * rb + r % rb, "col": c}),
+        (ca, lambda j: {"row": r, "col": ((c // cb + j) % ca) * cb + c % cb}),
     ):
         groups.append([(j, place(j)) for j in range(1, size)])
 
@@ -108,13 +150,12 @@
                     noff[k, p, d] = 4096
 
     for k in range(2):
-        for dr, dc, place in (
-            (-1, 0, (slice(None), pl.ds(0, HALO))),
-            (1, 0, (slice(None), pl.ds(HALO + WIN, HALO))),
-            (0, -1, (0, pl.ds(HALO, WIN))),
-            (0, 1, (3, pl.ds(HALO, WIN))),
+        for cond, place in (
+            (jnp.logical_not(has_outer), (slice(None), pl.ds(outer, HALO))),
+            (c == 0, (0, pl.ds(0, 512))),
+            (c == n_col - 1, (3, pl.ds(0, 512))),
         ):
-            @pl.when(jnp.logical_not(exists(dr, dc)))
+            @pl.when(cond)
             def _(k=k, place=place):
                 ref = spans[k].at[(slice(None),) + place + (slice(None),)]
                 ref[...] = jnp.zeros(ref.shape, f32)
@@ -143,57 +184,126 @@
     ]
     for copy in copies:
         copy.start()
+    copies[0].wait()
+    copies[1].wait()
 
     pl.semaphore_wait(barrier, total)
 
-    def remote(src, dst, send, recv, dr, dc):
-        return pltpu.make_async_remote_copy(
-            src, dst, send, recv, device_id={"row": r + dr, "col": c + dc}, device_id_type=MESH
+    def along(dc, src, dst, cond=None):
+        send_if, recv_if = col_ok(c + dc), col_ok(c - dc)
+        if cond is not None:
+            send_if, recv_if = send_if & cond(c), recv_if & cond(c - dc)
+        return Message(pool, {"row": r, "col": c + dc}, send_if, recv_if, src, dst)
+
+    def strip(dc, src, dst, start, count, relay, also=None):
+        edge = Z_LEN - 1 if dc > 0 else 0
+        one, two = dc - dc * Z_LEN, dc * Z_LEN
+        both = lambda f: f if also is None else (lambda x: f(x) & also)
+        inside = both(lambda x: x % Z_LEN != edge)
+        cross = both(lambda x: (x % Z_LEN == edge) & col_ok(x + dc))
+        rows = pl.ds(start, count)
+        whole = along(dc, src.at[:, rows, :], dst.at[:, rows, :], inside)
+        pairs = []
+        size = count // CHUNKS
+        for n in range(CHUNKS):
+            rows = pl.ds(start + n * size, size)
+            slot = relay.at[:, pl.ds(n * size, size), :]
+            pairs.append(
+                (
+                    along(one, src.at[:, rows, :], slot, cross),
+                    along(two, slot, dst.at[:, rows, :], lambda x: cross(x - one)),
+                )
+            )
+        return whole, pairs
+
+    def widen(k):
+        span = spans[k]
+        relays, direct, far_strips, rows_in, corners, corner_relays, cores = [], [], [], [], [], [], []
+        for i, (dc, here, there) in enumerate(((1, 2, 0), (-1, 1, 3))):
+            whole, pairs = strip(dc, span.at[:, here], span.at[:, there], far, HALF, relay_strip.at[k, i])
+            far_strips.append(whole)
+            relays += pairs
+            direct.append(
+                along(dc, span.at[:, here, pl.ds(near, HALF), :], span.at[:, there, pl.ds(near, HALF), :])
+            )
+            rows = pl.ds(outer, HALF // 2)
+            corners.append(
+                along(dc, span.at[:, here, rows, :], span.at[:, there, rows, :], lambda x: has_outer)
+            )
+            whole, pairs = strip(
+                dc, span.at[:, here], span.at[:, there], outer + HALF // 2, HALF // 2, relay_corner.at[k, i], has_outer
+            )
+            corners.append(whole)
+            corner_relays += pairs
+        mirrored_inner = (HALO + WIN) * odd
+        for t in (0, 3):
+            cores.append(
+                Message(
+                    pool, partner, None, None,
+                    span.at[:, t, pl.ds(near, HALF), :],
+                    span.at[:, t, pl.ds(pl.multiple_of(mirrored_inner, HALF), HALF), :],
+                )
+            )
+        both_tiles = pl.ds(1, 2)
+        rows_in.append(
+            Message(
+                pool, beyond, has_outer, has_outer,
+                span.at[:, both_tiles, pl.ds(far, HALF), :],
+                span.at[:, both_tiles, pl.ds(pl.multiple_of((HALO + WIN) * (1 - odd), HALF), HALF), :],
+            )
         )
-
-    def start(copy, dr, dc):
-        @pl.when(exists(dr, dc))
-        def _():
-            copy.start()
-
-    def finish(copy, dr, dc):
-        @pl.when(exists(dr, dc))
-        def _():
-            copy.wait_send()
-
-        @pl.when(exists(-dr, -dc))
-        def _():
-            copy.wait_recv()
-
-    def widen_col(k):
-        out_copies = []
-        for i, (dc, tile, there) in enumerate(((-1, 1, 3), (1, 2, 0))):
-            if k == 0:
-                src = spec.at[:, :, pl.ds((tile - 1) * HALF, HALF)]
-            else:
-                src = spans[k].at[:, tile, pl.ds(HALO, WIN), :]
-            dst = spans[k].at[:, there, pl.ds(HALO, WIN), :]
-            copy = remote(src, dst, span_send.at[k, i], span_recv.at[k, i], 0, dc)
-            start(copy, 0, dc)
-            out_copies.append((copy, 0, dc))
-        return out_copies
-
-    def widen_row(k):
-        out_copies = []
-        for i, (dr, here, there) in enumerate(((-1, HALO, HALO + WIN), (1, WIN, 0))):
-            src = spans[k].at[:, :, pl.ds(here, HALO), :]
-            dst = spans[k].at[:, :, pl.ds(there, HALO), :]
-            copy = remote(src, dst, span_send.at[k, 2 + i], span_recv.at[k, 2 + i], dr, 0)
-            start(copy, dr, 0)
-            out_copies.append((copy, dr, 0))
-        return out_copies
-
-    first = widen_col(0)
+        rows_in.append(
+            Message(
+                pool, partner, None, None,
+                span.at[:, both_tiles, pl.ds(near, HALF), :],
+                span.at[:, both_tiles, pl.ds(pl.multiple_of(mirrored_inner, HALF), HALF), :],
+            )
+        )
+        for first, _ in relays:
+            first.start()
+        for m in rows_in + direct + far_strips:
+            m.start()
+
+        def middle():
+            for first, second in relays:
+                first.recv()
+                second.start()
+            for m in rows_in:
+                m.recv()
+            for first, _ in corner_relays:
+                first.start()
+            for m in corners:
+                m.start()
+            for m in direct:
+                m.recv()
+            for m in cores:
+                m.start()
+            for first, second in corner_relays:
+                first.recv()
+                second.start()
+
+        def end():
+            for m in far_strips + cores + corners:
+                m.recv()
+            for _, second in relays + corner_relays:
+                second.recv()
+            for m in rows_in + direct + far_strips + cores + corners:
+                m.sent()
+            for first, second in relays + corner_relays:
+                first.sent()
+                second.sent()
+
+        return middle, end
+
+    middle, end = widen(0)
     off_copies = []
     for i, (dr, dc) in enumerate(NEIGHBOURS):
         slot = (-dr + 1) * 3 + (-dc + 1)
-        copy = remote(off.at[0, 0], noff.at[slot], off_sem.at[0, i], off_sem.at[1, i], dr, dc)
-        start(copy, dr, dc)
+        copy = pltpu.make_async_remote_copy(
+            off.at[0, 0], noff.at[slot], off_sem.at[0, i], off_sem.at[1, i],
+            device_id={"row": r + dr, "col": c + dc}, device_id_type=MESH,
+        )
+        pl.when(exists(dr, dc))(copy.start)
         off_copies.append((copy, dr, dc))
 
     def clear(ref, count):
@@ -205,8 +315,6 @@
 
     clear(pad, 7)
     copies[2].wait()
-    copies[0].wait()
-    copies[1].wait()
     for t in range(2):
         cols = pl.ds(t * HALF, HALF)
         pad[2 + t, pl.ds(WIN, WIN), :] = probe[0, :, cols] * probe[0, :, cols] + probe[1, :, cols] * probe[1, :, cols]
@@ -218,19 +326,18 @@
 
     lax.fori_loop(0, n_pos * 12, clear_wide, 0)
 
-    for item in first:
-        finish(*item)
-    second = widen_row(0)
-
-    for item in off_copies:
-        finish(*item)
+    middle()
+
+    for copy, dr, dc in off_copies:
+        pl.when(exists(dr, dc))(copy.wait_send)
+        pl.when(exists(-dr, -dc))(copy.wait_recv)
 
     light[...] = jnp.zeros(light.shape, f32)
 
     def add_light(i, _):
-        near, p = i // n_pos, i % n_pos
-        top = jnp.clip(noff[near, p, 0] + (near // 3 - 1) * WIN, -WIN, WIN)
-        side = jnp.clip(noff[near, p, 1] + (near % 3 - 1) * WIN, -WIN, WIN)
+        tile, p = i // n_pos, i % n_pos
+        top = jnp.clip(noff[tile, p, 0] + (tile // 3 - 1) * WIN, -WIN, WIN)
+        side = jnp.clip(noff[tile, p, 1] + (tile % 3 - 1) * WIN, -WIN, WIN)
         rows = pl.ds(WIN - top, WIN)
         start_col = WIN - side
         q, s = start_col // HALF, start_col % HALF
@@ -283,8 +390,7 @@
     peak = peak_finish(0, items)
     items = peak_start(1, peak)
 
-    for item in second:
-        finish(*item)
+    end()
 
     def cat(a, b, axis):
         return jnp.concatenate([a, b], axis=axis)
@@ -337,67 +443,137 @@
             wide[p, part, 3, pl.ds(WIN, WIN), :] = jnp.where(past, two, one)
             wide[p, part, 4, pl.ds(WIN, WIN), :] = jnp.where(past, zero, two)
 
-    def gather(k):
-        def body(i, _):
-            part, t = i // 4, i % 4
-            for chunk in range(4):
-                acc = None
-                for p in range(n_pos):
-                    top = off[0, 0, p, 0] + HALO
-                    q = (off[0, 0, p, 1] + HALO) // HALF
-                    piece = wide[p, part, 2 + t - q, pl.ds(WIN - top + chunk * HALF, HALF), :]
-                    acc = piece if acc is None else acc + piece
-                grad[k, part, t, pl.ds(chunk * HALF, HALF), :] = acc
-            return 0
-
-        lax.fori_loop(0, 8, body, 0)
+    tops = [off[0, 0, p, 0] + HALO for p in range(n_pos)]
+    tiles = [(off[0, 0, p, 1] + HALO) // HALF for p in range(n_pos)]
+
+    def gather(k, t, start):
+        for part in range(2):
+            acc = None
+            for p in range(n_pos):
+                piece = wide[p, part, 2 + t - tiles[p], pl.ds(WIN - tops[p] + start, HALF), :]
+                acc = piece if acc is None else acc + piece
+            grad[k, part, t, pl.ds(start, HALF), :] = acc
+
+    def accumulate(k, t, start, ref):
+        for part in range(2):
+            rows = pl.ds(start, HALF)
+            grad[k, part, t, rows, :] = grad[k, part, t, rows, :] + ref[part]
+
+    def fold(k, between):
+        g = grad.at[k]
+        relays, direct, far_strips, corners, corner_relays, cores = [], [], [], [], [], []
+        for i, (dc, here) in enumerate(((1, 3), (-1, 0))):
+            whole, pairs = strip(dc, g.at[:, here], col_in.at[k, i], far, HALF, relay_strip.at[ITERS + k, i])
+            far_strips.append(whole)
+            relays += pairs
+            direct.append(
+                along(dc, g.at[:, here, pl.ds(near, HALF), :], col_in.at[k, i, :, pl.ds(near, HALF), :])
+            )
+            rows = pl.ds(outer, HALF // 2)
+            corners.append(
+                along(dc, g.at[:, here, rows, :], corner_in.at[k, i, :, rows, :], lambda x: has_outer)
+            )
+            whole, pairs = strip(
+                dc, g.at[:, here], corner_in.at[k, i], outer + HALF // 2, HALF // 2,
+                relay_corner.at[ITERS + k, i], has_outer,
+            )
+            corners.append(whole)
+            corner_relays += pairs
+            cores.append(
+                Message(pool, partner, None, None, g.at[:, here, pl.ds(inner, HALF), :], core_in.at[k, i])
+            )
+        both_tiles = pl.ds(1, 2)
+        row_out = Message(
+            pool, beyond, has_outer, has_outer, g.at[:, both_tiles, pl.ds(outer, HALF), :], row_in.at[k, 0]
+        )
+        row_core = Message(pool, partner, None, None, g.at[:, both_tiles, pl.ds(inner, HALF), :], row_in.at[k, 1])
+
+        for t in (0, 3):
+            gather(k, t, outer)
+        for first, _ in corner_relays:
+            first.start()
+        for m in corners:
+            m.start()
+        for t in (0, 3):
+            gather(k, t, inner)
+        for m in cores:
+            m.start()
+        for t in (0, 3):
+            gather(k, t, far)
+        for first, _ in relays:
+            first.start()
+        for m in far_strips:
+            m.start()
+        for t in (0, 3):
+            gather(k, t, near)
+        for t in (1, 2):
+            gather(k, t, outer)
+        for i, m in enumerate(cores):
+            m.recv()
+            accumulate(k, (3, 0)[i], near, core_in.at[k, i])
+        for m in direct:
+            m.start()
+        for first, second in corner_relays:
+            first.recv()
+            second.start()
+        for t in (1, 2):
+            gather(k, t, inner)
+        row_core.start()
+        for first, second in relays:
+            first.recv()
+            second.start()
+        for m in corners:
+            m.recv()
+        for _, second in corner_relays:
+            second.recv()
+        for i in range(2):
+            @pl.when(has_outer & col_ok(c - (1, -1)[i]))
+            def _(i=i):
+                accumulate(k, 1 + i, outer, corner_in.at[k, i, :, pl.ds(outer, HALF), :])
+        row_out.start()
+        for t in (1, 2):
+            gather(k, t, near)
+            gather(k, t, far)
+        between()
+        row_core.recv()
+        for t in (1, 2):
+            accumulate(k, t, near, row_in.at[k, 1, :, t - 1])
+        for m in direct + far_strips:
+            m.recv()
+        for _, second in relays:
+            second.recv()
+        for i in range(2):
+            @pl.when(col_ok(c - (1, -1)[i]))
+            def _(i=i):
+                for start in (near, far):
+                    accumulate(k, 1 + i, start, col_in.at[k, i, :, pl.ds(start, HALF), :])
+        row_out.recv()
+
+        @pl.when(has_outer)
+        def _():
+            for t in (1, 2):
+                accumulate(k, t, far, row_in.at[k, 0, :, t - 1])
+
+        def end():
+            for m in [row_out, row_core] + direct + far_strips + corners + cores:
+                m.sent()
+            for first, second in relays + corner_relays:
+                first.sent()
+                second.sent()
+
+        return end
 
     for k in range(ITERS):
         lax.fori_loop(0, n_pos, lambda p, _, k=k: (window(k, p), 0)[1], 0)
-        gather(k)
-
-        sent = []
-        for i, (dr, here) in enumerate(((-1, 0), (1, HALO + WIN))):
-            copy = remote(
-                grad.at[k, :, :, pl.ds(here, HALO), :], row_in.at[k, i], fold_send.at[k, i], fold_recv.at[k, i], dr, 0
-            )
-            start(copy, dr, 0)
-            sent.append((copy, dr, 0))
-        if k == 0:
-            peak = peak_finish(1, items)
-            items = peak_start(2, peak)
-        for i, (copy, dr, dc) in enumerate(sent):
-            finish(copy, dr, dc)
-            rows = pl.ds(WIN, HALO) if dr < 0 else pl.ds(HALO, HALO)
-
-            @pl.when(exists(-dr, 0))
-            def _(i=i, rows=rows):
-                for part in range(2):
-                    for t in range(4):
-                        grad[k, part, t, rows, :] = grad[k, part, t, rows, :] + row_in[k, i, part, t]
-
-        sent = []
-        for i, (dc, here) in enumerate(((-1, 0), (1, 3))):
-            copy = remote(
-                grad.at[k, :, here, pl.ds(HALO, WIN), :], col_in.at[k, i],
-                fold_send.at[k, 2 + i], fold_recv.at[k, 2 + i], 0, dc,
-            )
-            start(copy, 0, dc)
-            sent.append((copy, 0, dc))
-        if k == 0:
-            peak = peak_finish(2, items)
-            items = peak_start(3, peak)
-            peak = jnp.max(peak_finish(3, items))
-            inv[...] = 1.0 / (light[...] + RIDGE * peak)
-        for i, (copy, dr, dc) in enumerate(sent):
-            finish(copy, dr, dc)
-            t = 2 if dc < 0 else 1
-
-            @pl.when(exists(0, -dc))
-            def _(i=i, t=t):
-                for part in range(2):
-                    grad[k, part, t, pl.ds(HALO, WIN), :] = grad[k, part, t, pl.ds(HALO, WIN), :] + col_in[k, i, part]
-
+
+        def between():
+            if k == 0:
+                value = peak_finish(1, items)
+                value = peak_finish(2, peak_start(2, value))
+                value = jnp.max(peak_finish(3, peak_start(3, value)))
+                inv[...] = 1.0 / (light[...] + RIDGE * value)
+
+        end = fold(k, between)
         for t in range(2):
             for part in range(2):
                 new = spans[k][part, 1 + t, pl.ds(HALO, WIN), :] - grad[k, part, 1 + t, pl.ds(HALO, WIN), :] * inv[t]
@@ -406,10 +582,10 @@
                 else:
                     out[part, :, pl.ds(t * HALF, HALF)] = new
         if k + 1 < ITERS:
-            for item in widen_col(k + 1):
-                finish(*item)
-            for item in widen_row(k + 1):
-                finish(*item)
+            middle, end_widen = widen(k + 1)
+            middle()
+            end_widen()
+        end()
 
 
 def solution(mesh):
@@ -443,16 +619,18 @@
                 vmem(n_pos, WIN, WIN),
                 pltpu.VMEM((10, WIN, WIN), jnp.bfloat16),
                 pltpu.SMEM((9, n_pos, 2), jnp.int32),
-                vmem(ITERS, 2, 2, 4, HALO, HALF),
-                vmem(ITERS, 2, 2, WIN, HALF),
+                vmem(ITERS, 2, 2, 512, HALF),
+                vmem(ITERS, 2, 2, HALF, HALF),
+                vmem(ITERS, 2, 2, 2, HALO, HALF),
+                vmem(ITERS, 2, 2, 512, HALF),
+                vmem(2 * ITERS, 2, 2, HALF, HALF),
+                vmem(2 * ITERS, 2, 2, HALF // 2, HALF),
                 vmem(4, 8, HALF),
                 vmem(4, 8, 8, HALF),
                 dma(5),
                 dma(2, 8),
-                dma(ITERS, 4),
-                dma(ITERS, 4),
-                dma(ITERS, 4),
-                dma(ITERS, 4),
+                dma(112),
+                dma(112),
                 dma(4, 8),
                 dma(4, 8),
             ],

time: 136 us -> 120 us (0.88)
  the two profiles are of different devices: /device:TPU:43 before, /device:TPU:25 now
where the time goes in v2:
time: 120 us
  Pallas kernels  117 us (98%)
  local copies, waits for them, and re-layouts  3.2 us (3%)
    pallas_call x1, Pallas kernels, local(): pl.pallas_call(functools.partial(kernel, n_row, n_col, n_pos), out_shape=...  117 us
    unnamed x2, local copies, waits for them, and re-layouts  3.2 us

profile of v2, /device:TPU:25, one launch (start us, length us, event | category | flops | bytes accessed | tf_op | source)
XLA Modules:
  0.0 120.1 jit_solution(8272498489624541454)
XLA Ops:
  0.0 1.3 %copy.6.off = s32[1,1,3,2]{3,2,1,0:T(4,128)} copy(s32[1,1,3,2]{2,3,1,0:T(2,128)} %param.7) | data formatting | bytes 48 | tf_op args[2]
  1.3 116.9 %shard_map.55 = f32[2,256,256]{2,1,0:T(8,128)} custom-call(f32[2,256,256]{2,1,0:T(8,128)} %spec.1, f32[2,256,256]{2,1,0:T(8,128)} %probe_in.1, s32[1,1,3,2]{3,2,1,0:T(4,128)} %copy.6.off, f32[1,1,3,256,256]{4,3,2,1,0:T(8,128)} %amp_in.1, bf16[10,256,256]{2,1,0:T(8,128)(2,1)} %constant.2.clone.tab_in), custom_call_target="tpu_custom_call" | custom-call | tf_op jit(solution)/shard_map/pallas_call | solution.py:599
  118.3 1.9 %copy.8 = f32[2,256,256]{2,1,0:T(8,128)} copy(f32[2,256,256]{2,1,0:T(8,128)} %shard_map.55) | data formatting | bytes 1048576

commit v3 on v2

--- a/solution.py
+++ b/solution.py
@@ -100,7 +100,7 @@
     spec, probe_in, off, amp_in, tab_in,
     out,
     span_a, span_b, grad, wide, pad, light, inv, probe, amp, tab, noff,
-    corner_in, core_in, row_in, col_in, relay_strip, relay_corner, peak_out, peak_in,
+    corner_in, core_in, row_in, col_in, relay_strip, relay_row, peak_out, peak_in,
     local_sem, off_sem, send_sem, recv_sem, peak_send, peak_recv,
 ):
     r, c = lax.axis_index("row"), lax.axis_index("col")
@@ -114,6 +114,7 @@
     far = pl.multiple_of(HALO + HALF * odd, HALF)
     inner = pl.multiple_of((HALO + WIN) * (1 - odd), HALF)
     outer = pl.multiple_of((HALO + WIN) * odd, HALF)
+    inner_there, outer_there = outer, inner
     partner = {"row": r + 1 - 2 * odd, "col": c}
     r_out = r - 1 + 2 * odd
     has_outer = (r_out >= 0) & (r_out < n_row)
@@ -145,9 +146,9 @@
         for p in range(n_pos):
             for d in range(2):
                 if k == 4:
-                    noff[k, p, d] = off[0, 0, p, d]
+                    noff[k, d, p] = off[0, 0, d, p]
                 else:
-                    noff[k, p, d] = 4096
+                    noff[k, d, p] = 4096
 
     for k in range(2):
         for cond, place in (
@@ -216,9 +217,39 @@
             )
         return whole, pairs
 
+    def planes(x):
+        return ((x % Z_LEN == Z_LEN - 1) & (x < n_col - 1)) | ((x % Z_LEN == 0) & (x > 0))
+
+    def outer_rows(src, dst, relay):
+        half, size = HALF // 2, HALF // 2 // CHUNKS
+        end_here = planes(c)
+        first_end = c % Z_LEN == 0
+        passes = ((c % Z_LEN == Z_LEN - 2) & planes(c + 1)) | ((c % Z_LEN == 1) & planes(c - 1))
+        to_relay = {"row": r, "col": c + jnp.where(first_end, 1, -1)}
+        from_relay = {"row": r_out, "col": c + jnp.where(c % Z_LEN == 1, -1, 1)}
+
+        def part(start, count, cond):
+            rows = pl.ds(start, count)
+            return Message(pool, beyond, cond, cond, src.at[:, :, rows, :], dst.at[:, :, rows, :])
+
+        direct = [part(0, half, has_outer), part(half, half, has_outer & jnp.logical_not(end_here))]
+        pairs = []
+        for n in range(CHUNKS):
+            rows = pl.ds(half + n * size, size)
+            slot = relay.at[:, :, pl.ds(n * size, size), :]
+            pairs.append(
+                (
+                    Message(pool, to_relay, has_outer & end_here, has_outer & passes, src.at[:, :, rows, :], slot),
+                    Message(pool, from_relay, has_outer & passes, has_outer & end_here, slot, dst.at[:, :, rows, :]),
+                )
+            )
+        return direct, pairs
+
+    both_tiles = pl.ds(1, 2)
+
     def widen(k):
         span = spans[k]
-        relays, direct, far_strips, rows_in, corners, corner_relays, cores = [], [], [], [], [], [], []
+        relays, direct, far_strips, corners, cores = [], [], [], [], []
         for i, (dc, here, there) in enumerate(((1, 2, 0), (-1, 1, 3))):
             whole, pairs = strip(dc, span.at[:, here], span.at[:, there], far, HALF, relay_strip.at[k, i])
             far_strips.append(whole)
@@ -226,76 +257,71 @@
             direct.append(
                 along(dc, span.at[:, here, pl.ds(near, HALF), :], span.at[:, there, pl.ds(near, HALF), :])
             )
-            rows = pl.ds(outer, HALF // 2)
+            rows = pl.ds(outer, HALF)
             corners.append(
                 along(dc, span.at[:, here, rows, :], span.at[:, there, rows, :], lambda x: has_outer)
             )
-            whole, pairs = strip(
-                dc, span.at[:, here], span.at[:, there], outer + HALF // 2, HALF // 2, relay_corner.at[k, i], has_outer
-            )
-            corners.append(whole)
-            corner_relays += pairs
-        mirrored_inner = (HALO + WIN) * odd
+        mirrored = pl.ds(inner_there, HALF)
         for t in (0, 3):
             cores.append(
                 Message(
-                    pool, partner, None, None,
-                    span.at[:, t, pl.ds(near, HALF), :],
-                    span.at[:, t, pl.ds(pl.multiple_of(mirrored_inner, HALF), HALF), :],
+                    pool, partner, None, None, span.at[:, t, pl.ds(near, HALF), :], span.at[:, t, mirrored, :]
                 )
             )
-        both_tiles = pl.ds(1, 2)
-        rows_in.append(
-            Message(
-                pool, beyond, has_outer, has_outer,
-                span.at[:, both_tiles, pl.ds(far, HALF), :],
-                span.at[:, both_tiles, pl.ds(pl.multiple_of((HALO + WIN) * (1 - odd), HALF), HALF), :],
-            )
+        row_core = Message(
+            pool, partner, None, None,
+            span.at[:, both_tiles, pl.ds(near, HALF), :], span.at[:, both_tiles, mirrored, :],
         )
-        rows_in.append(
-            Message(
-                pool, partner, None, None,
-                span.at[:, both_tiles, pl.ds(near, HALF), :],
-                span.at[:, both_tiles, pl.ds(pl.multiple_of(mirrored_inner, HALF), HALF), :],
-            )
+        row_far, row_relays = outer_rows(
+            span.at[:, both_tiles, pl.ds(far, HALF), :],
+            span.at[:, both_tiles, pl.ds(outer_there, HALF), :],
+            relay_row.at[k],
         )
-        for first, _ in relays:
-            first.start()
-        for m in rows_in + direct + far_strips:
-            m.start()
+
+        def start_far():
+            for first, _ in relays + row_relays:
+                first.start()
+            for m in row_far + far_strips:
+                m.start()
+
+        def start_near():
+            row_core.start()
+            for m in direct:
+                m.start()
+
+        def relay(n):
+            for pairs in (relays, row_relays):
+                for first, second in pairs[n::CHUNKS]:
+                    first.recv()
+                    second.start()
 
         def middle():
-            for first, second in relays:
-                first.recv()
-                second.start()
-            for m in rows_in:
+            for m in row_far:
                 m.recv()
-            for first, _ in corner_relays:
-                first.start()
+            for _, second in row_relays:
+                second.recv()
+            row_core.recv()
             for m in corners:
                 m.start()
             for m in direct:
                 m.recv()
             for m in cores:
                 m.start()
-            for first, second in corner_relays:
-                first.recv()
-                second.start()
 
         def end():
             for m in far_strips + cores + corners:
                 m.recv()
-            for _, second in relays + corner_relays:
+            for _, second in relays:
                 second.recv()
-            for m in rows_in + direct + far_strips + cores + corners:
+            for m in [row_core] + row_far + direct + far_strips + cores + corners:
                 m.sent()
-            for first, second in relays + corner_relays:
+            for first, second in relays + row_relays:
                 first.sent()
                 second.sent()
 
-        return middle, end
-
-    middle, end = widen(0)
+        return start_near, start_far, relay, middle, end
+
+    start_near, start_far, relay, middle, end = widen(0)
     off_copies = []
     for i, (dr, dc) in enumerate(NEIGHBOURS):
         slot = (-dr + 1) * 3 + (-dc + 1)
@@ -305,6 +331,8 @@
         )
         pl.when(exists(dr, dc))(copy.start)
         off_copies.append((copy, dr, dc))
+    start_far()
+    start_near()
 
     def clear(ref, count):
         def body(i, _):
@@ -324,10 +352,6 @@
         wide[p, rest // 6, rest % 6] = jnp.zeros((3 * WIN, HALF), f32)
         return 0
 
-    lax.fori_loop(0, n_pos * 12, clear_wide, 0)
-
-    middle()
-
     for copy, dr, dc in off_copies:
         pl.when(exists(dr, dc))(copy.wait_send)
         pl.when(exists(-dr, -dc))(copy.wait_recv)
@@ -336,8 +360,8 @@
 
     def add_light(i, _):
         tile, p = i // n_pos, i % n_pos
-        top = jnp.clip(noff[tile, p, 0] + (tile // 3 - 1) * WIN, -WIN, WIN)
-        side = jnp.clip(noff[tile, p, 1] + (tile % 3 - 1) * WIN, -WIN, WIN)
+        top = jnp.clip(noff[tile, 0, p] + (tile // 3 - 1) * WIN, -WIN, WIN)
+        side = jnp.clip(noff[tile, 1, p] + (tile % 3 - 1) * WIN, -WIN, WIN)
         rows = pl.ds(WIN - top, WIN)
         start_col = WIN - side
         q, s = start_col // HALF, start_col % HALF
@@ -348,7 +372,10 @@
             light[t] = light[t] + jnp.where(keep, rolled[t], rolled[t + 1])
         return 0
 
-    lax.fori_loop(0, 9 * n_pos, add_light, 0)
+    for n in range(3):
+        lax.fori_loop(3 * n * n_pos, 3 * (n + 1) * n_pos, add_light, 0)
+        if n < CHUNKS:
+            relay(n)
 
     peak = jnp.max(light[...].reshape(2 * WIN // 8, 8, HALF), axis=0)
 
@@ -373,6 +400,9 @@
         return value
 
     items = peak_start(0, peak)
+    middle()
+
+    lax.fori_loop(0, n_pos * 12, clear_wide, 0)
 
     copies[3].wait()
     copies[4].wait()
@@ -389,15 +419,14 @@
     lax.fori_loop(0, n_pos, order_amp, 0)
     peak = peak_finish(0, items)
     items = peak_start(1, peak)
-
     end()
 
     def cat(a, b, axis):
         return jnp.concatenate([a, b], axis=axis)
 
     def window(k, p):
-        top = off[0, 0, p, 0] + HALO
-        side = off[0, 0, p, 1] + HALO
+        top = off[0, 0, 0, p] + HALO
+        side = off[0, 0, 1, p] + HALO
         q, s = side // HALF, side % HALF
         rows = pl.ds(top, WIN)
         turn = (HALF - s) % HALF
@@ -443,8 +472,8 @@
             wide[p, part, 3, pl.ds(WIN, WIN), :] = jnp.where(past, two, one)
             wide[p, part, 4, pl.ds(WIN, WIN), :] = jnp.where(past, zero, two)
 
-    tops = [off[0, 0, p, 0] + HALO for p in range(n_pos)]
-    tiles = [(off[0, 0, p, 1] + HALO) // HALF for p in range(n_pos)]
+    tops = [off[0, 0, 0, p] + HALO for p in range(n_pos)]
+    tiles = [(off[0, 0, 1, p] + HALO) // HALF for p in range(n_pos)]
 
     def gather(k, t, start):
         for part in range(2):
@@ -459,9 +488,9 @@
             rows = pl.ds(start, HALF)
             grad[k, part, t, rows, :] = grad[k, part, t, rows, :] + ref[part]
 
-    def fold(k, between):
+    def fold(k, on_near, on_far):
         g = grad.at[k]
-        relays, direct, far_strips, corners, corner_relays, cores = [], [], [], [], [], []
+        relays, direct, far_strips, corners, cores = [], [], [], [], []
         for i, (dc, here) in enumerate(((1, 3), (-1, 0))):
             whole, pairs = strip(dc, g.at[:, here], col_in.at[k, i], far, HALF, relay_strip.at[ITERS + k, i])
             far_strips.append(whole)
@@ -469,29 +498,19 @@
             direct.append(
                 along(dc, g.at[:, here, pl.ds(near, HALF), :], col_in.at[k, i, :, pl.ds(near, HALF), :])
             )
-            rows = pl.ds(outer, HALF // 2)
             corners.append(
-                along(dc, g.at[:, here, rows, :], corner_in.at[k, i, :, rows, :], lambda x: has_outer)
-            )
-            whole, pairs = strip(
-                dc, g.at[:, here], corner_in.at[k, i], outer + HALF // 2, HALF // 2,
-                relay_corner.at[ITERS + k, i], has_outer,
-            )
-            corners.append(whole)
-            corner_relays += pairs
+                along(dc, g.at[:, here, pl.ds(outer, HALF), :], corner_in.at[k, i], lambda x: has_outer)
+            )
             cores.append(
                 Message(pool, partner, None, None, g.at[:, here, pl.ds(inner, HALF), :], core_in.at[k, i])
             )
-        both_tiles = pl.ds(1, 2)
-        row_out = Message(
-            pool, beyond, has_outer, has_outer, g.at[:, both_tiles, pl.ds(outer, HALF), :], row_in.at[k, 0]
+        row_far, row_relays = outer_rows(
+            g.at[:, both_tiles, pl.ds(outer, HALF), :], row_in.at[k, 0], relay_row.at[ITERS + k]
         )
         row_core = Message(pool, partner, None, None, g.at[:, both_tiles, pl.ds(inner, HALF), :], row_in.at[k, 1])
 
         for t in (0, 3):
             gather(k, t, outer)
-        for first, _ in corner_relays:
-            first.start()
         for m in corners:
             m.start()
         for t in (0, 3):
@@ -513,79 +532,109 @@
             accumulate(k, (3, 0)[i], near, core_in.at[k, i])
         for m in direct:
             m.start()
-        for first, second in corner_relays:
+        for t in (1, 2):
+            gather(k, t, inner)
+        row_core.start()
+        for i, m in enumerate(corners):
+            m.recv()
+
+            @pl.when(has_outer & col_ok(c - (1, -1)[i]))
+            def _(i=i):
+                accumulate(k, 1 + i, outer, corner_in.at[k, i])
+        for first, _ in row_relays:
+            first.start()
+        for m in row_far:
+            m.start()
+        for first, second in relays:
             first.recv()
             second.start()
         for t in (1, 2):
-            gather(k, t, inner)
-        row_core.start()
-        for first, second in relays:
+            gather(k, t, near)
+            gather(k, t, far)
+        for first, second in row_relays:
             first.recv()
             second.start()
-        for m in corners:
-            m.recv()
-        for _, second in corner_relays:
-            second.recv()
-        for i in range(2):
-            @pl.when(has_outer & col_ok(c - (1, -1)[i]))
-            def _(i=i):
-                accumulate(k, 1 + i, outer, corner_in.at[k, i, :, pl.ds(outer, HALF), :])
-        row_out.start()
-        for t in (1, 2):
-            gather(k, t, near)
-            gather(k, t, far)
-        between()
         row_core.recv()
         for t in (1, 2):
             accumulate(k, t, near, row_in.at[k, 1, :, t - 1])
-        for m in direct + far_strips:
+
+        def columns(start):
+            for i in range(2):
+                @pl.when(col_ok(c - (1, -1)[i]))
+                def _(i=i):
+                    accumulate(k, 1 + i, start, col_in.at[k, i, :, pl.ds(start, HALF), :])
+
+        for m in direct:
+            m.recv()
+        columns(near)
+        on_near()
+        for m in far_strips:
             m.recv()
         for _, second in relays:
             second.recv()
-        for i in range(2):
-            @pl.when(col_ok(c - (1, -1)[i]))
-            def _(i=i):
-                for start in (near, far):
-                    accumulate(k, 1 + i, start, col_in.at[k, i, :, pl.ds(start, HALF), :])
-        row_out.recv()
+        columns(far)
+        for m in row_far:
+            m.recv()
+        for _, second in row_relays:
+            second.recv()
 
         @pl.when(has_outer)
         def _():
             for t in (1, 2):
                 accumulate(k, t, far, row_in.at[k, 0, :, t - 1])
 
+        on_far()
+
         def end():
-            for m in [row_out, row_core] + direct + far_strips + corners + cores:
+            for m in [row_core] + row_far + direct + far_strips + corners + cores:
                 m.sent()
-            for first, second in relays + corner_relays:
+            for first, second in relays + row_relays:
                 first.sent()
                 second.sent()
 
         return end
 
-    for k in range(ITERS):
-        lax.fori_loop(0, n_pos, lambda p, _, k=k: (window(k, p), 0)[1], 0)
-
-        def between():
-            if k == 0:
-                value = peak_finish(1, items)
-                value = peak_finish(2, peak_start(2, value))
-                value = jnp.max(peak_finish(3, peak_start(3, value)))
-                inv[...] = 1.0 / (light[...] + RIDGE * value)
-
-        end = fold(k, between)
+    def update(k, start):
+        rows = pl.ds(start, HALF)
         for t in range(2):
             for part in range(2):
-                new = spans[k][part, 1 + t, pl.ds(HALO, WIN), :] - grad[k, part, 1 + t, pl.ds(HALO, WIN), :] * inv[t]
+                step = grad[k, part, 1 + t, rows, :] * inv[t, pl.ds(start - HALO, HALF), :]
+                new = spans[k][part, 1 + t, rows, :] - step
                 if k + 1 < ITERS:
-                    spans[k + 1][part, 1 + t, pl.ds(HALO, WIN), :] = new
+                    spans[k + 1][part, 1 + t, rows, :] = new
                 else:
-                    out[part, :, pl.ds(t * HALF, HALF)] = new
-        if k + 1 < ITERS:
-            middle, end_widen = widen(k + 1)
+                    out[part, pl.ds(start - HALO, HALF), pl.ds(t * HALF, HALF)] = new
+
+    for k in range(ITERS):
+        last = k + 1 == ITERS
+        for p in range(n_pos):
+            window(k, p)
+            if k == 0 and p < 3:
+                peak = peak_finish(1 + p, items)
+                if p < 2:
+                    items = peak_start(2 + p, peak)
+                else:
+                    inv[...] = 1.0 / (light[...] + RIDGE * jnp.max(peak))
+        if not last:
+            start_near, start_far, relay, middle, end = widen(k + 1)
+
+        def on_near():
+            update(k, near)
+            if not last:
+                start_near()
+
+        def on_far():
+            update(k, far)
+            if not last:
+                start_far()
+
+        end_fold = fold(k, on_near, on_far)
+        if not last:
+            for n in range(CHUNKS):
+                relay(n)
             middle()
-            end_widen()
-        end()
+            end()
+        end_fold()
 
 
 def solution(mesh):
@@ -618,8 +667,8 @@
                 vmem(2, WIN, WIN),
                 vmem(n_pos, WIN, WIN),
                 pltpu.VMEM((10, WIN, WIN), jnp.bfloat16),
-                pltpu.SMEM((9, n_pos, 2), jnp.int32),
-                vmem(ITERS, 2, 2, 512, HALF),
+                pltpu.SMEM((9, 2, n_pos), jnp.int32),
+                vmem(ITERS, 2, 2, HALF, HALF),
                 vmem(ITERS, 2, 2, HALF, HALF),
                 vmem(ITERS, 2, 2, 2, HALO, HALF),
                 vmem(ITERS, 2, 2, 512, HALF),
@@ -637,7 +686,7 @@
             compiler_params=pltpu.CompilerParams(
                 collective_id=0, has_side_effects=True, vmem_limit_bytes=56 * 1024 * 1024
             ),
-        )(specimen, probe_field, offsets, amplitudes, jnp.asarray(tables))
+        )(specimen, probe_field, jnp.swapaxes(offsets, 2, 3), amplitudes, jnp.asarray(tables))
 
     return jax.shard_map(
         local,

time: 120 us -> 108 us (0.900)
  the two profiles are of different devices: /device:TPU:25 before, /device:TPU:21 now
where the time goes in v3:
time: 108 us
  Pallas kernels  106 us (98%)
  local copies, waits for them, and re-layouts  1.87 us (2%)
    pallas_call x1, Pallas kernels, local(): pl.pallas_call(functools.partial(kernel, n_row, n_col, n_pos), out_shape=...  106 us

profile of v3, /device:TPU:21, one launch (start us, length us, event | category | flops | bytes accessed | tf_op | source)
XLA Modules:
  0.0 107.8 jit_solution(8132936508616649103)
XLA Ops:
  0.0 106.0 %shard_map.55 = f32[2,256,256]{2,1,0:T(8,128)} custom-call(f32[2,256,256]{2,1,0:T(8,128)} %spec.1, f32[2,256,256]{2,1,0:T(8,128)} %probe_in.1, s32[1,1,2,3]{3,2,1,0:T(2,128)} %bitcast.1, f32[1,1,3,256,256]{4,3,2,1,0:T(8,128)} %amp_in.1, bf16[10,256,256]{2,1,0:T(8,128)(2,1)} %constant.2.clone.tab_in), custom_call_target="tpu_custom_call" | custom-call | tf_op jit(solution)/shard_map/pallas_call | solution.py:648
  106.0 1.9 %copy.7 = f32[2,256,256]{2,1,0:T(8,128)} copy(f32[2,256,256]{2,1,0:T(8,128)} %shard_map.55) | data formatting | bytes 1048576

commit v4 on v3

--- a/solution.py
+++ b/solution.py
@@ -352,30 +352,37 @@
         wide[p, rest // 6, rest % 6] = jnp.zeros((3 * WIN, HALF), f32)
         return 0
 
+    lax.fori_loop(0, n_pos * 12, clear_wide, 0)
+    for n in range(CHUNKS):
+        relay(n)
     for copy, dr, dc in off_copies:
         pl.when(exists(dr, dc))(copy.wait_send)
         pl.when(exists(-dr, -dc))(copy.wait_recv)
 
     light[...] = jnp.zeros(light.shape, f32)
 
-    def add_light(i, _):
-        tile, p = i // n_pos, i % n_pos
-        top = jnp.clip(noff[tile, 0, p] + (tile // 3 - 1) * WIN, -WIN, WIN)
-        side = jnp.clip(noff[tile, 1, p] + (tile % 3 - 1) * WIN, -WIN, WIN)
-        rows = pl.ds(WIN - top, WIN)
-        start_col = WIN - side
-        q, s = start_col // HALF, start_col % HALF
-        turn = (HALF - s) % HALF
-        rolled = [pltpu.roll(pad[q + j, rows, :], turn, 1) for j in range(3)]
-        keep = lane < HALF - s
-        for t in range(2):
-            light[t] = light[t] + jnp.where(keep, rolled[t], rolled[t + 1])
-        return 0
-
-    for n in range(3):
-        lax.fori_loop(3 * n * n_pos, 3 * (n + 1) * n_pos, add_light, 0)
-        if n < CHUNKS:
-            relay(n)
+    for dr, dc in [(0, 0)] + NEIGHBOURS:
+        place = (dr + 1) * 3 + dc + 1
+        first, count = {-1: (0, HALF), 0: (0, WIN), 1: (HALF, HALF)}[dr]
+        tiles_in = {-1: (0,), 0: (0, 1), 1: (1,)}[dc]
+
+        def add_light(p, _, place=place, dr=dr, dc=dc, first=first, count=count, tiles_in=tiles_in):
+            top = jnp.clip(noff[place, 0, p] + dr * WIN, -WIN, WIN)
+            side = jnp.clip(noff[place, 1, p] + dc * WIN, -WIN, WIN)
+            rows = pl.ds(WIN - top + first, count)
+            start_col = WIN - side
+            q, s = start_col // HALF, start_col % HALF
+            turn = (HALF - s) % HALF
+            keep = lane < HALF - s
+            rolled = {
+                j: pltpu.roll(pad[q + j, rows, :], turn, 1) for j in range(tiles_in[0], tiles_in[-1] + 2)
+            }
+            here = pl.ds(first, count)
+            for t in tiles_in:
+                light[t, here, :] = light[t, here, :] + jnp.where(keep, rolled[t], rolled[t + 1])
+            return 0
+
+        lax.fori_loop(0, n_pos, add_light, 0)
 
     peak = jnp.max(light[...].reshape(2 * WIN // 8, 8, HALF), axis=0)
 
@@ -401,8 +408,6 @@
 
     items = peak_start(0, peak)
     middle()
-
-    lax.fori_loop(0, n_pos * 12, clear_wide, 0)
 
     copies[3].wait()
     copies[4].wait()
@@ -424,56 +429,66 @@
     def cat(a, b, axis):
         return jnp.concatenate([a, b], axis=axis)
 
-    def window(k, p):
-        top = off[0, 0, 0, p] + HALO
-        side = off[0, 0, 1, p] + HALO
-        q, s = side // HALF, side % HALF
-        rows = pl.ds(top, WIN)
-        turn = (HALF - s) % HALF
-        keep = lane < HALF - s
-        patch = []
-        for part in range(2):
-            rolled = [
-                pltpu.roll(spans[k][part, jnp.minimum(q + j, 3), rows, :], turn, 1) for j in range(3)
-            ]
-            patch.append(cat(jnp.where(keep, rolled[0], rolled[1]), jnp.where(keep, rolled[1], rolled[2]), 1))
+    def windows(k):
+        every = range(n_pos)
         pr, pi = probe[0], probe[1]
-        er = pr * patch[0] - pi * patch[1]
-        ei = pr * patch[1] + pi * patch[0]
-        sums = cat(er[:HALF] + er[HALF:], ei[:HALF] + ei[HALF:], 0)
-        difs = cat(er[:HALF] - er[HALF:], ei[:HALF] - ei[HALF:], 0)
-        even = left(tab, 0, sums)
-        odd = left(tab, 1, difs)
-        xr = cat(even[:HALF], odd[:HALF], 0)
-        xi = cat(even[HALF:], odd[HALF:], 0)
-        sums = cat(xr[:, :HALF] + xr[:, HALF:], xi[:, :HALF] + xi[:, HALF:], 1)
-        difs = cat(xr[:, :HALF] - xr[:, HALF:], xi[:, :HALF] - xi[:, HALF:], 1)
-        out_cols = []
-        for index, x in ((0, sums), (1, difs)):
-            far = right(x, tab, 2 + index)
-            fr, fi = far[:, :HALF], far[:, HALF:]
-            factor = 1.0 - amp[p, :, pl.ds(index * HALF, HALF)] * lax.rsqrt(fr * fr + fi * fi + SMOOTH)
-            out_cols.append(right(cat(factor * fr, factor * fi, 1), tab, index))
-        lo, hi = out_cols[0] + out_cols[1], out_cols[0] - out_cols[1]
-        xr = cat(lo[:, :HALF], hi[:, :HALF], 1)
-        xi = cat(lo[:, HALF:], hi[:, HALF:], 1)
-        even = left(tab, 2, cat(xr[:HALF], xi[:HALF], 0))
-        odd = left(tab, 3, cat(xr[HALF:], xi[HALF:], 0))
-        lo, hi = even + odd, even - odd
-        br = cat(lo[:HALF], hi[:HALF], 0)
-        bi = cat(lo[HALF:], hi[HALF:], 0)
-        g = (pr * br + pi * bi, pr * bi - pi * br)
-        past = lane >= s
+        shift = [side % HALF for side in sides]
+        sums, difs = [], []
+        for p in every:
+            rows = pl.ds(tops[p], WIN)
+            turn = (HALF - shift[p]) % HALF
+            keep = lane < HALF - shift[p]
+            patch = []
+            for part in range(2):
+                rolled = [
+                    pltpu.roll(spans[k][part, jnp.minimum(tiles[p] + j, 3), rows, :], turn, 1) for j in range(3)
+                ]
+                patch.append(cat(jnp.where(keep, rolled[0], rolled[1]), jnp.where(keep, rolled[1], rolled[2]), 1))
+            er = pr * patch[0] - pi * patch[1]
+            ei = pr * patch[1] + pi * patch[0]
+            sums.append(cat(er[:HALF] + er[HALF:], ei[:HALF] + ei[HALF:], 0))
+            difs.append(cat(er[:HALF] - er[HALF:], ei[:HALF] - ei[HALF:], 0))
+        even = [left(tab, 0, x) for x in sums]
+        odd_ = [left(tab, 1, x) for x in difs]
+        sums, difs = [], []
+        for p in every:
+            xr = cat(even[p][:HALF], odd_[p][:HALF], 0)
+            xi = cat(even[p][HALF:], odd_[p][HALF:], 0)
+            sums.append(cat(xr[:, :HALF] + xr[:, HALF:], xi[:, :HALF] + xi[:, HALF:], 1))
+            difs.append(cat(xr[:, :HALF] - xr[:, HALF:], xi[:, :HALF] - xi[:, HALF:], 1))
+        back = []
+        for index, xs in ((0, sums), (1, difs)):
+            far_field = [right(x, tab, 2 + index) for x in xs]
+            scaled = []
+            for p in every:
+                fr, fi = far_field[p][:, :HALF], far_field[p][:, HALF:]
+                factor = 1.0 - amp[p, :, pl.ds(index * HALF, HALF)] * lax.rsqrt(fr * fr + fi * fi + SMOOTH)
+                scaled.append(cat(factor * fr, factor * fi, 1))
+            back.append([right(x, tab, index) for x in scaled])
+        even, odd_ = [], []
+        for p in every:
+            lo, hi = back[0][p] + back[1][p], back[0][p] - back[1][p]
+            xr = cat(lo[:, :HALF], hi[:, :HALF], 1)
+            xi = cat(lo[:, HALF:], hi[:, HALF:], 1)
+            even.append(left(tab, 2, cat(xr[:HALF], xi[:HALF], 0)))
+            odd_.append(left(tab, 3, cat(xr[HALF:], xi[HALF:], 0)))
         zero = jnp.zeros((WIN, HALF), f32)
-        for part in range(2):
-            one = pltpu.roll(g[part][:, :HALF], s, 1)
-            two = pltpu.roll(g[part][:, HALF:], s, 1)
-            wide[p, part, 2, pl.ds(WIN, WIN), :] = jnp.where(past, one, zero)
-            wide[p, part, 3, pl.ds(WIN, WIN), :] = jnp.where(past, two, one)
-            wide[p, part, 4, pl.ds(WIN, WIN), :] = jnp.where(past, zero, two)
+        for p in every:
+            lo, hi = even[p] + odd_[p], even[p] - odd_[p]
+            br = cat(lo[:HALF], hi[:HALF], 0)
+            bi = cat(lo[HALF:], hi[HALF:], 0)
+            g = (pr * br + pi * bi, pr * bi - pi * br)
+            past = lane >= shift[p]
+            for part in range(2):
+                one = pltpu.roll(g[part][:, :HALF], shift[p], 1)
+                two = pltpu.roll(g[part][:, HALF:], shift[p], 1)
+                wide[p, part, 2, pl.ds(WIN, WIN), :] = jnp.where(past, one, zero)
+                wide[p, part, 3, pl.ds(WIN, WIN), :] = jnp.where(past, two, one)
+                wide[p, part, 4, pl.ds(WIN, WIN), :] = jnp.where(past, zero, two)
 
     tops = [off[0, 0, 0, p] + HALO for p in range(n_pos)]
-    tiles = [(off[0, 0, 1, p] + HALO) // HALF for p in range(n_pos)]
+    sides = [off[0, 0, 1, p] + HALO for p in range(n_pos)]
+    tiles = [side // HALF for side in sides]
 
     def gather(k, t, start):
         for part in range(2):
@@ -488,7 +503,7 @@
             rows = pl.ds(start, HALF)
             grad[k, part, t, rows, :] = grad[k, part, t, rows, :] + ref[part]
 
-    def fold(k, on_near, on_far):
+    def fold(k, before, on_near, on_far):
         g = grad.at[k]
         relays, direct, far_strips, corners, cores = [], [], [], [], []
         for i, (dc, here) in enumerate(((1, 3), (-1, 0))):
@@ -554,6 +569,7 @@
         for first, second in row_relays:
             first.recv()
             second.start()
+        before()
         row_core.recv()
         for t in (1, 2):
             accumulate(k, t, near, row_in.at[k, 1, :, t - 1])
@@ -607,14 +623,18 @@
 
     for k in range(ITERS):
         last = k + 1 == ITERS
-        for p in range(n_pos):
-            window(k, p)
-            if k == 0 and p < 3:
-                peak = peak_finish(1 + p, items)
-                if p < 2:
-                    items = peak_start(2 + p, peak)
-                else:
-                    inv[...] = 1.0 / (light[...] + RIDGE * jnp.max(peak))
+        if k == 0:
+            peak = peak_finish(1, items)
+            items = peak_start(2, peak)
+        windows(k)
+        if k == 0:
+            peak = peak_finish(2, items)
+            items = peak_start(3, peak)
+
+        def before():
+            if k == 0:
+                inv[...] = 1.0 / (light[...] + RIDGE * jnp.max(peak_finish(3, items)))
+
         if not last:
             start_near, start_far, relay, middle, end = widen(k + 1)
 
@@ -628,7 +648,7 @@
             if not last:
                 start_far()
 
-        end_fold = fold(k, on_near, on_far)
+        end_fold = fold(k, before, on_near, on_far)
         if not last:
             for n in range(CHUNKS):
                 relay(n)

time: 108 us -> 98.4 us (0.911)
  the two profiles are of different devices: /device:TPU:21 before, /device:TPU:35 now
where the time goes in v4:
time: 98.4 us; the launch traced here: 98.2 us
  Pallas kernels  96.3 us (98%)
  local copies, waits for them, and re-layouts  1.87 us (2%)
    pallas_call x1, Pallas kernels, local(): pl.pallas_call(functools.partial(kernel, n_row, n_col, n_pos), out_shape=...  96.3 us

profile of v4, /device:TPU:35, one launch (start us, length us, event | category | flops | bytes accessed | tf_op | source)
XLA Modules:
  0.0 98.2 jit_solution(13938682484477888437)
XLA Ops:
  0.0 96.3 %shard_map.55 = f32[2,256,256]{2,1,0:T(8,128)} custom-call(f32[2,256,256]{2,1,0:T(8,128)} %spec.1, f32[2,256,256]{2,1,0:T(8,128)} %probe_in.1, s32[1,1,2,3]{3,2,1,0:T(2,128)} %bitcast.1, f32[1,1,3,256,256]{4,3,2,1,0:T(8,128)} %amp_in.1, bf16[10,256,256]{2,1,0:T(8,128)(2,1)} %constant.2.clone.tab_in), custom_call_target="tpu_custom_call" | custom-call | tf_op jit(solution)/shard_map/pallas_call | solution.py:668
  96.3 1.9 %copy.7 = f32[2,256,256]{2,1,0:T(8,128)} copy(f32[2,256,256]{2,1,0:T(8,128)} %shard_map.55) | data formatting | bytes 1048576

commit v5 on v4

--- a/solution.py
+++ b/solution.py
@@ -352,7 +352,6 @@
         wide[p, rest // 6, rest % 6] = jnp.zeros((3 * WIN, HALF), f32)
         return 0
 
-    lax.fori_loop(0, n_pos * 12, clear_wide, 0)
     for n in range(CHUNKS):
         relay(n)
     for copy, dr, dc in off_copies:
@@ -408,6 +407,8 @@
 
     items = peak_start(0, peak)
     middle()
+
+    lax.fori_loop(0, n_pos * 12, clear_wide, 0)
 
     copies[3].wait()
     copies[4].wait()
@@ -550,6 +551,9 @@
         for t in (1, 2):
             gather(k, t, inner)
         row_core.start()
+        for first, second in relays:
+            first.recv()
+            second.start()
         for i, m in enumerate(corners):
             m.recv()
 
@@ -560,9 +564,6 @@
             first.start()
         for m in row_far:
             m.start()
-        for first, second in relays:
-            first.recv()
-            second.start()
         for t in (1, 2):
             gather(k, t, near)
             gather(k, t, far)

time: 98.4 us -> 100 us (1.016)
  the two profiles are of different devices: /device:TPU:35 before, /device:TPU:43 now
where the time goes in v5:
time: 100 us
  Pallas kernels  98.2 us (98%)
  local copies, waits for them, and re-layouts  1.87 us (2%)
    pallas_call x1, Pallas kernels, local(): pl.pallas_call(functools.partial(kernel, n_row, n_col, n_pos), out_shape=...  98.2 us

profile of v5, /device:TPU:43, one launch (start us, length us, event | category | flops | bytes accessed | tf_op | source)
XLA Modules:
  0.0 100.1 jit_solution(12620142960450129546)
XLA Ops:
  0.0 98.2 %shard_map.55 = f32[2,256,256]{2,1,0:T(8,128)} custom-call(f32[2,256,256]{2,1,0:T(8,128)} %spec.1, f32[2,256,256]{2,1,0:T(8,128)} %probe_in.1, s32[1,1,2,3]{3,2,1,0:T(2,128)} %bitcast.1, f32[1,1,3,256,256]{4,3,2,1,0:T(8,128)} %amp_in.1, bf16[10,256,256]{2,1,0:T(8,128)(2,1)} %constant.2.clone.tab_in), custom_call_target="tpu_custom_call" | custom-call | tf_op jit(solution)/shard_map/pallas_call | solution.py:669
  98.2 1.9 %copy.7 = f32[2,256,256]{2,1,0:T(8,128)} copy(f32[2,256,256]{2,1,0:T(8,128)} %shard_map.55) | data formatting | bytes 1048576
